TPU v7x, 256 devices: a whole 4x4x8 slice. The times are simulated.
256 devices in a mesh: wide: 16 (over y, x_hi, core), blk: 16 (over x_lo, z).
Axes of the slice: x: 4 (x_hi: 2, x_lo: 2; x = x_hi * 2 + x_lo), y: 4, z: 8, core: 2. Of those that a mesh axis runs over, the one named last changes fastest.
Arguments:
- lam: bfloat16 [512, 768, 768], P('blk', 'wide'), may hold values from -6 to 6
- ints: bfloat16 [768, 768, 2, 768], P('wide', 'blk'), may hold values from -0.0078125 to 0.0078125
Outputs:
- ladder: float32 [512, 2, 768], P(('wide', 'blk'))
All inputs are finite; a program needn't handle non-finite values.
Results may differ from a plain program's by a relative error of at most 0.0003.
Values may be sent and summed in bfloat16 or wider, within the bound.
No kernel may reach another device: no remote copies, remote signals or barrier semaphores. Data moves between devices by JAX's collectives and lax.ppermute only.
A program may use at most 128 MiB of HBM per device.

v0:
```python
import jax
import jax.numpy as jnp
from jax import lax
from jax.sharding import PartitionSpec as P


def shards(lam, ints):
    received = lax.all_to_all(lam, "blk", split_axis=2, concat_axis=0, tiled=True)
    pairs = received.shape[0]
    c_local = ints.shape[0]
    d_local = ints.shape[1]
    slab = ints.shape[2]
    virt = ints.shape[3]
    flat_lam = received.reshape(pairs, c_local * d_local)
    flat_ints = ints.reshape(c_local * d_local, slab * virt)
    owned = pairs // (lax.axis_size("wide") * lax.axis_size("blk"))
    product = jnp.dot(flat_lam, flat_ints, preferred_element_type=jnp.float32)
    return lax.psum_scatter(
        (0.5 * product).reshape(owned * lax.axis_size(("wide", "blk")), slab, virt),
        ("wide", "blk"),
        scatter_dimension=0,
        tiled=True,
    )


def solution(mesh):
    in_specs = (P("blk", "wide", None), P("wide", "blk", None, None))
    out_specs = P(("wide", "blk"), None, None)
    return jax.shard_map(shards, mesh=mesh, in_specs=in_specs, out_specs=out_specs, check_vma=False)
```

profile of v0, /device:TPU:1, one launch (start us, length us, event | category | flops | bytes accessed | tf_op | source)
XLA Modules:
  0.0 402.0 jit_solution(14467750569690303706)
XLA Ops:
  6.5 9.9 %copy.4 = bf16[32,48,768]{1,0,2:T(8,128)(2,1)} copy(bf16[32,48,768]{2,1,0:T(8,128)(2,1)} %param.2) | data formatting | bytes 4718592 | tf_op args[0]
  16.4 11.4 %reshape.13 = bf16[16,2,36864]{2,1,0:T(2,128)(2,1)} reshape(bf16[768,32,48]{2,1,0:T(8,128)(2,1)} %bitcast.13) | data formatting | bytes 4718592
  27.8 10.0 %all-to-all-start = ((bf16[16,2,36864]{2,1,0:T(2,128)(2,1)}), bf16[16,2,36864]{2,1,0:T(2,128)(2,1)S(1)}, u32[]{:S(2)}, u32[]{:S(2)}) async-start(bf16[16,2,36864]{2,1,0:T(2,128)(2,1)} %reshape.13), calls=%async_computation | async-start | bytes 4718592 | tf_op jit(solution)/shard_map/all_to_all | solution.py:8
  37.9 0.0 all-reduce.3.cloned.1.call-start
  37.9 7.2 %copy.6 = bf16[288,8,2,768]{3,1,2,0:T(8,128)(2,1)} copy(bf16[288,8,2,768]{3,2,1,0:T(2,128)(2,1)} %bitcast.14) | data formatting | bytes 14155776
  45.1 46.8 %all-to-all-done = bf16[16,2,36864]{2,1,0:T(2,128)(2,1)S(1)} async-done(((bf16[16,2,36864]{2,1,0:T(2,128)(2,1)}), bf16[16,2,36864]{2,1,0:T(2,128)(2,1)S(1)}, u32[]{:S(2)}, u32[]{:S(2)}) %all-to-all-start) | async-done | bytes 2359328 | tf_op jit(solution)/shard_map/all_to_all | solution.py:8
  91.9 7.4 %reshape.14 = bf16[768,32,48]{2,1,0:T(8,128)(2,1)} reshape(bf16[16,2,36864]{2,1,0:T(2,128)(2,1)S(1)} %all-to-all-done) | data formatting | bytes 4718592
  99.3 10.3 %copy.5 = bf16[32,48,16,48]{3,1,0,2:T(8,128)(2,1)} copy(bf16[32,48,16,48]{1,0,3,2:T(8,128)(2,1)} %bitcast.11) | data formatting | bytes 4718592 | tf_op jit(solution)/shard_map/all_to_all | solution.py:8
  109.6 9.6 %reshape.10 = bf16[512,2304]{1,0:T(8,128)(2,1)} reshape(bf16[16,32,48,48]{3,2,1,0:T(8,128)(2,1)} %bitcast.12) | data formatting | bytes 4718592 | tf_op jit(solution)/shard_map/reshape | solution.py:14
  119.2 6.8 %convolution_multiply_fusion = f32[512,1536]{1,0:T(8,128)S(1)} fusion(bf16[512,2304]{1,0:T(8,128)(2,1)} %reshape.10, bf16[2304,1536]{1,0:T(8,128)(2,1)} %bitcast.15), kind=kOutput, calls=%fused_computation | convolution fusion | flops 3624665088 | bytes 12582912 | tf_op jit(solution)/shard_map/dot_general | solution.py:17
  126.0 3.3 reshape.12
  129.3 0.0 all-reduce.3.cloned.1.call-update
  129.3 264.6 %all-reduce.3.cloned.1.call-done = f32[512,2,768]{2,1,0:T(2,128)} async-done(((f32[512,2,768]{2,1,0:T(2,128)}), f32[512,2,768]{2,1,0:T(2,128)}) %all-reduce.3.cloned.1.call-update) | async-done | bytes 3145744
  393.9 1.3 constant_dynamic-slice_fusion
Async XLA Ops:
  27.8 64.0 %all-to-all-start = ((bf16[16,2,36864]{2,1,0:T(2,128)(2,1)}), bf16[16,2,36864]{2,1,0:T(2,128)(2,1)S(1)}, u32[]{:S(2)}, u32[]{:S(2)}) async-start(bf16[16,2,36864]{2,1,0:T(2,128)(2,1)} %reshape.13), calls=%async_computation | async-start | bytes 4718592 | tf_op jit(solution)/shard_map/all_to_all | solution.py:8
  37.9 356.0 %all-reduce.3.cloned.1.call-start = ((), (), s32[]{:S(2)}) async-start(), calls=%async_computation.1 | async-start | bytes 6291456
Sparse Core Ops, SparseCore 0:
  129.4 264.4 all-reduce.2
where the time goes:
time: 404 us; the launch traced here: 402 us
  waiting for transfers between devices  311 us (77%)
  local copies, waits for them, and re-layouts  60.4 us (15%)
  between operations  13.4 us (3%)
  starting transfers between devices  10.1 us (2%)
  matrix products  6.77 us (2%)
    unnamed x2, waiting for transfers between devices  265 us
    all_to_all x1, waiting for transfers between devices, shards(): lax.all_to_all(lam, 'blk', split_axis=2, concat_axis=0, tiled=True)  46.8 us
    unnamed x5, local copies, waits for them, and re-layouts  37.2 us
    all_to_all x1, local copies, waits for them, and re-layouts, shards(): lax.all_to_all(lam, 'blk', split_axis=2, concat_axis=0, tiled=True)  10.3 us
    all_to_all x1, starting transfers between devices, shards(): lax.all_to_all(lam, 'blk', split_axis=2, concat_axis=0, tiled=True)  10 us
    reshape x1, local copies, waits for them, and re-layouts, shards(): flat_lam = received.reshape(pairs, c_local * d_local)  9.63 us
  transfers between devices with their start and end apart: 2, of which 2 were waited for; matrix products, arithmetic and copies ran while one was open for 2% of the time, Pallas kernels for 0%

commit v1 on v0

v1 whole, which is shorter than its diff:
```python
import jax
import jax.numpy as jnp
from jax import lax
from jax.experimental import pallas as pl
from jax.experimental.pallas import tpu as pltpu
from jax.sharding import Mesh, PartitionSpec as P

AXES = ("y", "xh", "core", "xl", "z")
SIZES = (4, 2, 2, 2, 8)
MIB = 1024 * 1024


def pack_kernel(lam_ref, out_ref, pick_ref):
    @pl.when(pl.program_id(0) == 0)
    def _():
        rows = lax.broadcasted_iota(jnp.int32, (512, 512), 0)
        cols = lax.broadcasted_iota(jnp.int32, (512, 512), 1)
        wanted = (2 * (rows % 16) + (rows // 16) % 2) * 16 + rows // 32
        pick_ref[...] = jnp.where(cols == wanted, 1.0, 0.0).astype(jnp.bfloat16)

    x = lam_ref[...].reshape(512, 768)
    y = jnp.dot(pick_ref[...], x, preferred_element_type=jnp.float32).astype(jnp.bfloat16)
    y = y.reshape(16, 2, 16, 768)
    for core in range(2):
        for j in range(16):
            out_ref[core * 16 + j] = jnp.concatenate(
                [y[c, core, :, 48 * j : 48 * j + 48] for c in range(16)], axis=-1
            )


def pack(lam):
    return pl.pallas_call(
        pack_kernel,
        grid=(3,),
        in_specs=[pl.BlockSpec((32, 16, 768), lambda m: (0, m, 0))],
        out_specs=pl.BlockSpec((32, 16, 768), lambda m: (0, 0, m)),
        out_shape=jax.ShapeDtypeStruct((32, 16, 2304), jnp.bfloat16),
        scratch_shapes=[pltpu.VMEM((512, 512), jnp.bfloat16)],
        compiler_params=pltpu.CompilerParams(vmem_limit_bytes=60 * MIB),
        cost_estimate=pl.CostEstimate(flops=3 * 2 * 512 * 512 * 768, bytes_accessed=4 * 1179648, transcendentals=0),
        name="pack",
    )(lam)


def product_kernel(core_ref, x_ref, w_own_ref, w_oth_ref, out_ref, held, acc_ref, sems):
    depth, steps = 384, 6
    copies = []
    for s, w in enumerate((w_own_ref, w_oth_ref)):
        for k in range(steps):
            copies.append(pltpu.make_async_copy(w.at[pl.ds(k * depth, depth)], held.at[s, k], sems.at[s, k]))
            copies[-1].start()
    core = core_ref[0]
    for s in range(2):
        x = x_ref.at[core if s == 0 else 1 - core]
        for k in range(steps):
            copies[s * steps + k].wait()
            lhs = x[:, :, k * depth : (k + 1) * depth].reshape(256, depth)
            for n in range(0, 1536, 512):
                term = jnp.dot(lhs, held[s, k, :, n : n + 512], preferred_element_type=jnp.float32)
                if s + k == 0:
                    acc_ref[:, n : n + 512] = term
                elif s * steps + k < 2 * steps - 1:
                    acc_ref[:, n : n + 512] += term
                else:
                    acc = (0.5 * (acc_ref[:, n : n + 512] + term)).reshape(8, 2, 2, 8, 512)
                    for c in range(2):
                        for x1 in range(2):
                            out_ref[:, x1, c, :, n : n + 512] = acc[:, c, x1]


def product(core, received, w_own, w_oth):
    return pl.pallas_call(
        product_kernel,
        in_specs=[
            pl.BlockSpec(memory_space=pltpu.SMEM),
            pl.BlockSpec(memory_space=pltpu.VMEM),
            pl.BlockSpec(memory_space=pl.ANY),
            pl.BlockSpec(memory_space=pl.ANY),
        ],
        out_specs=pl.BlockSpec(memory_space=pltpu.VMEM),
        out_shape=jax.ShapeDtypeStruct((8, 2, 2, 8, 1536), jnp.float32),
        scratch_shapes=[
            pltpu.VMEM((2, 6, 384, 1536), jnp.bfloat16),
            pltpu.VMEM((256, 1536), jnp.float32),
            pltpu.SemaphoreType.DMA((2, 6)),
        ],
        compiler_params=pltpu.CompilerParams(vmem_limit_bytes=20 * MIB),
        cost_estimate=pl.CostEstimate(flops=2 * 256 * 4608 * 1536, bytes_accessed=18 * MIB, transcendentals=0),
        name="product",
    )(core, received.reshape(2, 16, 16, 2304), *[pltpu.with_memory_space_constraint(w, pltpu.HBM) for w in (w_own, w_oth)])


def shards(lam, ints):
    core = lax.axis_index("core").astype(jnp.int32).reshape(1)
    ints_oth = lax.ppermute(ints, "core", [(0, 1), (1, 0)])
    w_own, w_oth = ints.reshape(2304, 1536), ints_oth.reshape(2304, 1536)
    received = lax.all_to_all(pack(lam), ("core", "xl", "z"), 0, 0)
    part = product(core, received, w_own, w_oth).reshape(16, 16, 1536)
    part = lax.all_to_all(part, ("y", "xh", "xl"), 0, 0).sum(0)
    part = lax.all_to_all(part.reshape(16, 12, 128), ("core", "z"), 0, 0)
    return part.reshape(2, 8, 12, 128).sum(1).reshape(2, 2, 768)


def solution(mesh):
    fine = Mesh(mesh.devices.reshape(SIZES), AXES)
    wide, blk = AXES[:3], AXES[3:]
    in_specs = (P(blk, wide, None), P(wide, blk, None, None))
    out_specs = P(AXES, None, None)
    return jax.shard_map(shards, mesh=fine, in_specs=in_specs, out_specs=out_specs, check_vma=False)
```

time: 404 us -> 122 us (0.30)
  waiting for transfers between devices: 311 us -> 39.8 us
  local copies, waits for them, and re-layouts: 60.4 us -> 14.9 us
  blocking collectives: 0 us -> 42.9 us
  between operations: 13.4 us -> 0.04 us
  Pallas kernels: 0 us -> 12.5 us
  matrix products: 6.77 us -> 0 us
    unnamed x2 -> x0, waiting for transfers between devices: 265 us -> none
    all_to_all x0 -> x2, blocking collectives: none -> 42.9 us  [the longest x1 28.4 us: shards(): part = lax.all_to_all(part, ('y', 'xh', 'xl'), 0, 0).sum(0)]
    unnamed x5 -> x2, local copies, waits for them, and re-layouts: 37.2 us -> 14.2 us
    pallas_call x0 -> x2, Pallas kernels: none -> 12.5 us  [the longest x1 6.95 us: product(): pl.pallas_call(product_kernel, in_specs=[pl.BlockSpec(memory_space=pltpu....]
    reshape x2, local copies, waits for them, and re-layouts: 12.9 us -> 0.63 us  [the longest x1 0.61 us: shards(): return part.reshape(2, 8, 12, 128).sum(1).reshape(2, 2, 768)]
    all_to_all x1 -> x0, local copies, waits for them, and re-layouts: 10.3 us -> none  [shards(): lax.all_to_all(lam, 'blk', split_axis=2, concat_axis=0, tiled=True)]
    all_to_all x1, waiting for transfers between devices: 46.8 us -> 39.8 us  [shards(): received = lax.all_to_all(pack(lam), ('core', 'xl', 'z'), 0, 0)]
    dot_general x1 -> x0, matrix products: 6.77 us -> none  [shards(): product = jnp.dot(flat_lam, flat_ints, preferred_element_type=jnp.float32)]
  transfers between devices with their start and end apart: 2 -> 2, of which waited for: 2 -> 1; matrix products, arithmetic and copies ran while one was open for 2% -> 12% of each run, Pallas kernels for 0% -> 5%
where the time goes in v1:
time: 122 us; the launch traced here: 121 us
  blocking collectives  42.9 us (35%)
  waiting for transfers between devices  39.8 us (33%)
  local copies, waits for them, and re-layouts  14.9 us (12%)
  Pallas kernels  12.5 us (10%)
  starting transfers between devices  11.2 us (9%)
    all_to_all x1, waiting for transfers between devices, shards(): received = lax.all_to_all(pack(lam), ('core', 'xl', 'z'), 0, 0)  39.8 us
    all_to_all x1, blocking collectives, shards(): part = lax.all_to_all(part, ('y', 'xh', 'xl'), 0, 0).sum(0)  28.4 us
    all_to_all x1, blocking collectives, shards(): part = lax.all_to_all(part.reshape(16, 12, 128), ('core', 'z'), 0, 0)  14.5 us
    unnamed x2, local copies, waits for them, and re-layouts  14.2 us
    all_to_all x1, starting transfers between devices, shards(): received = lax.all_to_all(pack(lam), ('core', 'xl', 'z'), 0, 0)  7.93 us
    pallas_call x1, Pallas kernels, product(): pl.pallas_call(product_kernel, in_specs=[pl.BlockSpec(memory_space=pltpu....  6.95 us
    pallas_call x1, Pallas kernels, pack(): pl.pallas_call(pack_kernel, grid=(3,), in_specs=[pl.BlockSpec((32, 16, 76...  5.53 us
    ppermute x1, starting transfers between devices, shards(): ints_oth = lax.ppermute(ints, 'core', [(0, 1), (1, 0)])  3.24 us
  transfers between devices with their start and end apart: 2, of which 1 were waited for; matrix products, arithmetic and copies ran while one was open for 12% of the time, Pallas kernels for 5%

profile of v1, /device:TPU:1, one launch (start us, length us, event | category | flops | bytes accessed | tf_op | source)
XLA Modules:
  0.0 121.4 jit_solution(16245876798453524571)
XLA Ops:
  0.0 3.2 %collective-permute-start = (bf16[48,48,2,768]{3,2,1,0:T(2,128)(2,1)}, bf16[48,48,2,768]{3,2,1,0:T(2,128)(2,1)}, u32[]{:S(2)}, u32[]{:S(2)}) collective-permute-start(bf16[48,48,2,768]{3,2,1,0:T(2,128)(2,1)} %param.3), channel_id=1, source_target_pairs={{0,16},{16,0},{1,17},{17,1},{2,18},{18,2},{3,19},{19,3},{4,20},{20... | collective-permute-start | bytes 21233672 | tf_op jit(solution)/shard_map/ppermute | solution.py:95
  3.2 5.5 %pack.1 = bf16[32,16,2304]{2,1,0:T(8,128)(2,1)} custom-call(bf16[32,48,768]{2,1,0:T(8,128)(2,1)} %lam_ref.1), custom_call_target="tpu_custom_call" | custom-call | flops 1207959552 | bytes 4718592 | tf_op jit(solution)/shard_map/pack/pallas_call | solution.py:32
  8.8 7.9 %all-to-all-start = ((bf16[32,16,2304]{2,1,0:T(8,128)(2,1)}), bf16[32,16,2304]{2,1,0:T(8,128)(2,1)S(1)}, u32[]{:S(2)}, u32[]{:S(2)}) async-start(bf16[32,16,2304]{2,1,0:T(8,128)(2,1)} %pack.1), calls=%async_computation | async-start | bytes 4718592 | tf_op jit(solution)/shard_map/all_to_all | solution.py:97
  16.7 7.2 %copy.3 = bf16[288,8,2,768]{3,1,2,0:T(8,128)(2,1)} copy(bf16[288,8,2,768]{3,2,1,0:T(2,128)(2,1)} %bitcast.15) | data formatting | bytes 14155776
  23.9 0.0 collective-permute-done
  23.9 7.1 %copy.4 = bf16[288,8,2,768]{3,1,2,0:T(8,128)(2,1)} copy(bf16[288,8,2,768]{3,2,1,0:T(2,128)(2,1)} %bitcast.8) | data formatting | bytes 14155776
  30.9 39.8 %all-to-all-done = bf16[32,16,2304]{2,1,0:T(8,128)(2,1)S(1)} async-done(((bf16[32,16,2304]{2,1,0:T(8,128)(2,1)}), bf16[32,16,2304]{2,1,0:T(8,128)(2,1)S(1)}, u32[]{:S(2)}, u32[]{:S(2)}) %all-to-all-start) | async-done | bytes 2359328 | tf_op jit(solution)/shard_map/all_to_all | solution.py:97
  70.8 6.9 %product.1 = f32[8,2,2,8,1536]{4,3,2,1,0:T(8,128)S(1)} custom-call(s32[1]{0:T(128)} %bitcast.core_ref, bf16[2,16,16,2304]{3,2,1,0:T(8,128)(2,1)S(1)} %bitcast.11, bf16[2304,1536]{1,0:T(8,128)(2,1)} %bitcast.13, bf16[2304,1536]{1,0:T(8,128)(2,1)} %bitcast.14), custom_call_target="tpu_custom_call" | custom-call | flops 3623878656 | bytes 18874368 | tf_op jit(solution)/shard_map/product/pallas_call | solution.py:72
  77.7 28.4 %all_to_all.15 = f32[16,16,1536]{2,1,0:T(8,128)S(1)} all-to-all(f32[16,16,1536]{2,1,0:T(8,128)S(1)} %bitcast.12), channel_id=1, replica_groups=mesh['y'=4,'xh'=2,'core'=2,'xl'=2,'z'=8] {'y','xh','xl'}, dimensions={0} | all-to-all | bytes 3145728 | tf_op jit(solution)/shard_map/all_to_all | solution.py:99
  106.1 0.1 reduce_sum.18
  106.3 14.5 %all_to_all.16 = f32[16,12,128]{2,1,0:T(8,128)S(1)} all-to-all(f32[16,12,128]{2,1,0:T(8,128)S(1)} %reshape.29), channel_id=1, replica_groups=mesh['y'=4,'xh'=2,'core'=2,'xl'=2,'z'=8] {'core','z'}, dimensions={0} | all-to-all | bytes 196608 | tf_op jit(solution)/shard_map/all_to_all | solution.py:100
  120.8 0.6 reshape.31
  (2 shorter events, 0.0 us)
Async XLA Ops:
  0.0 23.9 %collective-permute-start = (bf16[48,48,2,768]{3,2,1,0:T(2,128)(2,1)}, bf16[48,48,2,768]{3,2,1,0:T(2,128)(2,1)}, u32[]{:S(2)}, u32[]{:S(2)}) collective-permute-start(bf16[48,48,2,768]{3,2,1,0:T(2,128)(2,1)} %param.3), channel_id=1, source_target_pairs={{0,16},{16,0},{1,17},{17,1},{2,18},{18,2},{3,19},{19,3},{4,20},{20... | collective-permute-start | bytes 21233672 | tf_op jit(solution)/shard_map/ppermute | solution.py:95
  8.8 62.0 %all-to-all-start = ((bf16[32,16,2304]{2,1,0:T(8,128)(2,1)}), bf16[32,16,2304]{2,1,0:T(8,128)(2,1)S(1)}, u32[]{:S(2)}, u32[]{:S(2)}) async-start(bf16[32,16,2304]{2,1,0:T(8,128)(2,1)} %pack.1), calls=%async_computation | async-start | bytes 4718592 | tf_op jit(solution)/shard_map/all_to_all | solution.py:97

commit v2 on v1

--- a/solution.py
+++ b/solution.py
@@ -1,3 +1,5 @@
+import itertools
+
 import jax
 import jax.numpy as jnp
 from jax import lax
@@ -42,33 +44,41 @@
     )(lam)
 
 
-def product_kernel(core_ref, x_ref, w_own_ref, w_oth_ref, out_ref, held, acc_ref, sems):
-    depth, steps = 384, 6
+DEPTH = 256
+STEPS = 2304 // DEPTH
+
+
+def product_kernel(at_ref, x_ref, w_own_ref, w_oth_ref, *rest):
+    outs, (held, acc_ref, sems) = rest[:4], rest[4:]
     copies = []
     for s, w in enumerate((w_own_ref, w_oth_ref)):
-        for k in range(steps):
-            copies.append(pltpu.make_async_copy(w.at[pl.ds(k * depth, depth)], held.at[s, k], sems.at[s, k]))
+        for k in range(STEPS):
+            copies.append(pltpu.make_async_copy(w.at[pl.ds(k * DEPTH, DEPTH)], held.at[s, k], sems.at[s, k]))
             copies[-1].start()
-    core = core_ref[0]
+    core, me = at_ref[0], at_ref[1]
     for s in range(2):
         x = x_ref.at[core if s == 0 else 1 - core]
-        for k in range(steps):
-            copies[s * steps + k].wait()
-            lhs = x[:, :, k * depth : (k + 1) * depth].reshape(256, depth)
+        for k in range(STEPS):
+            copies[s * STEPS + k].wait()
+            lhs = x[:, :, k * DEPTH : (k + 1) * DEPTH].reshape(256, DEPTH)
             for n in range(0, 1536, 512):
                 term = jnp.dot(lhs, held[s, k, :, n : n + 512], preferred_element_type=jnp.float32)
                 if s + k == 0:
                     acc_ref[:, n : n + 512] = term
-                elif s * steps + k < 2 * steps - 1:
+                else:
                     acc_ref[:, n : n + 512] += term
-                else:
-                    acc = (0.5 * (acc_ref[:, n : n + 512] + term)).reshape(8, 2, 2, 8, 512)
-                    for c in range(2):
-                        for x1 in range(2):
-                            out_ref[:, x1, c, :, n : n + 512] = acc[:, c, x1]
+    for flip, out_ref in enumerate(outs):
+        for j in range(4):
+            gone = me ^ flip
+            y = jnp.where(core == 0, gone, j)
+            x = jnp.where(core == 0, j, gone)
+            for c in range(2):
+                row = (((y * 2 + x // 2) * 2 + c) * 2 + x % 2) * 8
+                out_ref[j, 8 * c : 8 * c + 8] = 0.5 * acc_ref[pl.ds(pl.multiple_of(row, 8), 8), :]
 
 
-def product(core, received, w_own, w_oth):
+def product(at, received, w_own, w_oth):
+    in_hbm = [pltpu.with_memory_space_constraint(w, pltpu.HBM) for w in (w_own, w_oth)]
     return pl.pallas_call(
         product_kernel,
         in_specs=[
@@ -77,28 +87,48 @@
             pl.BlockSpec(memory_space=pl.ANY),
             pl.BlockSpec(memory_space=pl.ANY),
         ],
-        out_specs=pl.BlockSpec(memory_space=pltpu.VMEM),
-        out_shape=jax.ShapeDtypeStruct((8, 2, 2, 8, 1536), jnp.float32),
+        out_specs=[pl.BlockSpec(memory_space=pltpu.VMEM)] * 4,
+        out_shape=[jax.ShapeDtypeStruct((4, 16, 1536), jnp.float32)] * 4,
         scratch_shapes=[
-            pltpu.VMEM((2, 6, 384, 1536), jnp.bfloat16),
+            pltpu.VMEM((2, STEPS, DEPTH, 1536), jnp.bfloat16),
             pltpu.VMEM((256, 1536), jnp.float32),
-            pltpu.SemaphoreType.DMA((2, 6)),
+            pltpu.SemaphoreType.DMA((2, STEPS)),
         ],
         compiler_params=pltpu.CompilerParams(vmem_limit_bytes=20 * MIB),
         cost_estimate=pl.CostEstimate(flops=2 * 256 * 4608 * 1536, bytes_accessed=18 * MIB, transcendentals=0),
         name="product",
-    )(core, received.reshape(2, 16, 16, 2304), *[pltpu.with_memory_space_constraint(w, pltpu.HBM) for w in (w_own, w_oth)])
+    )(at, received.reshape(2, 16, 16, 2304), *in_hbm)
+
+
+def pairs(flip, first):
+    out = []
+    for y, x, core in itertools.product(range(4), range(4), range(2)):
+        to_y, to_x = (y ^ flip, x) if core == first else (y, x ^ flip)
+        out.append(tuple(((b * 2 + a // 2) * 2 + core) * 2 + a % 2 for b, a in ((y, x), (to_y, to_x))))
+    return out
+
+
+def moved(piece, flip, first):
+    return lax.ppermute(piece, ("y", "xh", "core", "xl"), pairs(flip, first))
 
 
 def shards(lam, ints):
-    core = lax.axis_index("core").astype(jnp.int32).reshape(1)
+    core = lax.axis_index("core").astype(jnp.int32)
+    y, x = lax.axis_index("y").astype(jnp.int32), lax.axis_index(("xh", "xl")).astype(jnp.int32)
+    early, late = jnp.where(core == 0, y, x), jnp.where(core == 0, x, y)
     ints_oth = lax.ppermute(ints, "core", [(0, 1), (1, 0)])
     w_own, w_oth = ints.reshape(2304, 1536), ints_oth.reshape(2304, 1536)
     received = lax.all_to_all(pack(lam), ("core", "xl", "z"), 0, 0)
-    part = product(core, received, w_own, w_oth).reshape(16, 16, 1536)
-    part = lax.all_to_all(part, ("y", "xh", "xl"), 0, 0).sum(0)
-    part = lax.all_to_all(part.reshape(16, 12, 128), ("core", "z"), 0, 0)
-    return part.reshape(2, 8, 12, 128).sum(1).reshape(2, 2, 768)
+    part = product(jnp.stack([core, early]), received, w_own, w_oth)
+    total = part[0]
+    for flip in (2, 1, 3):
+        total = total + moved(part[flip], flip, 0)
+    pieces = [lax.dynamic_index_in_dim(total, late ^ flip, 0, keepdims=False) for flip in range(4)]
+    total = pieces[0]
+    for flip in (2, 1, 3):
+        total = total + moved(pieces[flip], flip, 1)
+    total = lax.all_to_all(total.reshape(16, 12, 128), ("core", "z"), 0, 0)
+    return total.reshape(2, 8, 12, 128).sum(1).reshape(2, 2, 768)
 
 
 def solution(mesh):

time: 122 us -> 116 us (0.951)
  blocking collectives: 42.9 us -> 15.2 us
  waiting for transfers between devices: 39.8 us -> 53.9 us
  starting transfers between devices: 11.2 us -> 18 us
    all_to_all x2 -> x1, blocking collectives: 42.9 us -> 15.2 us  [shards(): total = lax.all_to_all(total.reshape(16, 12, 128), ('core', 'z'), 0, 0)]
    ppermute x0 -> x6, waiting for transfers between devices: none -> 14.2 us  [moved(): return lax.ppermute(piece, ('y', 'xh', 'core', 'xl'), pairs(flip, first))]
    ppermute x0 -> x6, starting transfers between devices: none -> 6.82 us  [moved(): return lax.ppermute(piece, ('y', 'xh', 'core', 'xl'), pairs(flip, first))]
  transfers between devices with their start and end apart: 2 -> 8, of which waited for: 1 -> 7; matrix products, arithmetic and copies ran while one was open for 12% -> 12% of each run, Pallas kernels for 5% -> 5%
where the time goes in v2:
time: 116 us; the launch traced here: 115 us
  waiting for transfers between devices  53.9 us (46%)
  starting transfers between devices  18 us (16%)
  blocking collectives  15.2 us (13%)
  local copies, waits for them, and re-layouts  14.9 us (13%)
  Pallas kernels  13 us (11%)
    all_to_all x1, waiting for transfers between devices, shards(): received = lax.all_to_all(pack(lam), ('core', 'xl', 'z'), 0, 0)  39.8 us
    all_to_all x1, blocking collectives, shards(): total = lax.all_to_all(total.reshape(16, 12, 128), ('core', 'z'), 0, 0)  15.2 us
    unnamed x2, local copies, waits for them, and re-layouts  14.2 us
    ppermute x6, waiting for transfers between devices, moved(): return lax.ppermute(piece, ('y', 'xh', 'core', 'xl'), pairs(flip, first))  14.2 us
    all_to_all x1, starting transfers between devices, shards(): received = lax.all_to_all(pack(lam), ('core', 'xl', 'z'), 0, 0)  7.93 us
    pallas_call x1, Pallas kernels, product(): pl.pallas_call(product_kernel, in_specs=[pl.BlockSpec(memory_space=pltpu....  7.44 us
    ppermute x6, starting transfers between devices, moved(): return lax.ppermute(piece, ('y', 'xh', 'core', 'xl'), pairs(flip, first))  6.82 us
    pallas_call x1, Pallas kernels, pack(): pl.pallas_call(pack_kernel, grid=(3,), in_specs=[pl.BlockSpec((32, 16, 76...  5.51 us
  transfers between devices with their start and end apart: 8, of which 7 were waited for; matrix products, arithmetic and copies ran while one was open for 12% of the time, Pallas kernels for 5%

profile of v2, /device:TPU:1, one launch (start us, length us, event | category | flops | bytes accessed | tf_op | source)
XLA Modules:
  0.0 115.3 jit_solution(11422262774317246)
XLA Ops:
  0.0 3.2 %collective-permute-start = (bf16[48,48,2,768]{3,2,1,0:T(2,128)(2,1)}, bf16[48,48,2,768]{3,2,1,0:T(2,128)(2,1)}, u32[]{:S(2)}, u32[]{:S(2)}) collective-permute-start(bf16[48,48,2,768]{3,2,1,0:T(2,128)(2,1)} %param.3), channel_id=1, source_target_pairs={{0,16},{16,0},{1,17},{17,1},{2,18},{18,2},{3,19},{19,3},{4,20},{20... | collective-permute-start | bytes 21233672 | tf_op jit(solution)/shard_map/ppermute | solution.py:119
  3.2 5.5 %pack.1 = bf16[32,16,2304]{2,1,0:T(8,128)(2,1)} custom-call(bf16[32,48,768]{2,1,0:T(8,128)(2,1)} %lam_ref.1), custom_call_target="tpu_custom_call" | custom-call | flops 1207959552 | bytes 4718592 | tf_op jit(solution)/shard_map/pack/pallas_call | solution.py:34
  8.8 7.9 %all-to-all-start = ((bf16[32,16,2304]{2,1,0:T(8,128)(2,1)}), bf16[32,16,2304]{2,1,0:T(8,128)(2,1)S(1)}, u32[]{:S(2)}, u32[]{:S(2)}) async-start(bf16[32,16,2304]{2,1,0:T(8,128)(2,1)} %pack.1), calls=%async_computation | async-start | bytes 4718592 | tf_op jit(solution)/shard_map/all_to_all | solution.py:121
  16.7 7.2 %copy.3 = bf16[288,8,2,768]{3,1,2,0:T(8,128)(2,1)} copy(bf16[288,8,2,768]{3,2,1,0:T(2,128)(2,1)} %bitcast.26) | data formatting | bytes 14155776
  23.9 0.1 pad_add_fusion.at_ref
  24.0 0.0 collective-permute-done
  24.0 7.1 %copy.4 = bf16[288,8,2,768]{3,1,2,0:T(8,128)(2,1)} copy(bf16[288,8,2,768]{3,2,1,0:T(2,128)(2,1)} %bitcast.12) | data formatting | bytes 14155776
  31.0 39.8 %all-to-all-done = bf16[32,16,2304]{2,1,0:T(8,128)(2,1)S(1)} async-done(((bf16[32,16,2304]{2,1,0:T(8,128)(2,1)}), bf16[32,16,2304]{2,1,0:T(8,128)(2,1)S(1)}, u32[]{:S(2)}, u32[]{:S(2)}) %all-to-all-start) | async-done | bytes 2359328 | tf_op jit(solution)/shard_map/all_to_all | solution.py:121
  70.8 7.4 %product.1 = (f32[4,16,1536]{2,1,0:T(8,128)S(1)}, f32[4,16,1536]{2,1,0:T(8,128)S(1)}, f32[4,16,1536]{2,1,0:T(8,128)}, f32[4,16,1536]{2,1,0:T(8,128)S(1)}) custom-call(s32[2]{0:T(128)S(1)} %pad_add_fusion.at_ref, bf16[2,16,16,2304]{3,2,1,0:T(8,128)(2,1)S(1)} %bitcast.23, bf16[2304,1536]{1,0:T(8,128)(2,1)} %bitcast.24, bf16[2304,1536]{1,0:T(8,128)(2,1)} %bitcast.25), custom_call_target="tpu_custom_call" | custom-call | flops 3623878656 | bytes 18874368 | tf_op jit(solution)/shard_map/product/pallas_call | solution.py:82
  78.2 2.5 %collective-permute-start.1 = (f32[4,16,1536]{2,1,0:T(8,128)}, f32[4,16,1536]{2,1,0:T(8,128)S(1)}, u32[]{:S(2)}, u32[]{:S(2)}) collective-permute-start(f32[4,16,1536]{2,1,0:T(8,128)} %get-tuple-element.10), channel_id=1, source_target_pairs={{0,128},{16,48},{8,136},{24,56},{32,160},{48,16},{40,168},{56,24},... | collective-permute-start | bytes 1179656 | tf_op jit(solution)/shard_map/ppermute | solution.py:112
  80.8 0.0 collective-permute-start.2
  80.8 0.8 collective-permute-start.3
  81.6 5.4 %collective-permute-done.1 = f32[4,16,1536]{2,1,0:T(8,128)S(1)} collective-permute-done((f32[4,16,1536]{2,1,0:T(8,128)}, f32[4,16,1536]{2,1,0:T(8,128)S(1)}, u32[]{:S(2)}, u32[]{:S(2)}) %collective-permute-start.1) | collective-permute-done | bytes 393248 | tf_op jit(solution)/shard_map/ppermute | solution.py:112
  87.0 3.0 %collective-permute-done.2 = f32[4,16,1536]{2,1,0:T(8,128)S(1)} collective-permute-done((f32[4,16,1536]{2,1,0:T(8,128)S(1)}, f32[4,16,1536]{2,1,0:T(8,128)S(1)}, u32[]{:S(2)}, u32[]{:S(2)}) %collective-permute-start.2) | collective-permute-done | bytes 393248 | tf_op jit(solution)/shard_map/ppermute | solution.py:112
  89.9 1.2 %collective-permute-done.3 = f32[4,16,1536]{2,1,0:T(8,128)S(1)} collective-permute-done((f32[4,16,1536]{2,1,0:T(8,128)S(1)}, f32[4,16,1536]{2,1,0:T(8,128)S(1)}, u32[]{:S(2)}, u32[]{:S(2)}) %collective-permute-start.3) | collective-permute-done | bytes 393248 | tf_op jit(solution)/shard_map/ppermute | solution.py:112
  91.2 0.1 add_add_fusion
  91.3 2.7 %collective-permute-start.4 = (f32[16,1536]{1,0:T(8,128)S(1)}, f32[16,1536]{1,0:T(8,128)S(1)}, u32[]{:S(2)}, u32[]{:S(2)}) collective-permute-start(f32[16,1536]{1,0:T(8,128)S(1)} %get-tuple-element.13), channel_id=1, source_target_pairs={{0,32},{16,144},{8,40},{24,152},{32,0},{48,176},{40,8},{56,184},{6... | collective-permute-start | bytes 294920 | tf_op jit(solution)/shard_map/ppermute | solution.py:112
  94.0 0.7 collective-permute-start.5
  94.7 0.1 collective-permute-start.6
  94.8 1.6 %collective-permute-done.4 = f32[16,1536]{1,0:T(8,128)S(1)} collective-permute-done((f32[16,1536]{1,0:T(8,128)S(1)}, f32[16,1536]{1,0:T(8,128)S(1)}, u32[]{:S(2)}, u32[]{:S(2)}) %collective-permute-start.4) | collective-permute-done | bytes 98336 | tf_op jit(solution)/shard_map/ppermute | solution.py:112
  96.3 1.7 %collective-permute-done.5 = f32[16,1536]{1,0:T(8,128)S(1)} collective-permute-done((f32[16,1536]{1,0:T(8,128)S(1)}, f32[16,1536]{1,0:T(8,128)S(1)}, u32[]{:S(2)}, u32[]{:S(2)}) %collective-permute-start.5) | collective-permute-done | bytes 98336 | tf_op jit(solution)/shard_map/ppermute | solution.py:112
  98.0 1.3 %collective-permute-done.6 = f32[16,1536]{1,0:T(8,128)S(1)} collective-permute-done((f32[16,1536]{1,0:T(8,128)S(1)}, f32[16,1536]{1,0:T(8,128)S(1)}, u32[]{:S(2)}, u32[]{:S(2)}) %collective-permute-start.6) | collective-permute-done | bytes 98336 | tf_op jit(solution)/shard_map/ppermute | solution.py:112
  99.4 15.2 %all_to_all.10 = f32[16,12,128]{2,1,0:T(8,128)S(1)} all-to-all(f32[16,12,128]{2,1,0:T(8,128)S(1)} %reshape.21), channel_id=1, replica_groups=mesh['y'=4,'xh'=2,'core'=2,'xl'=2,'z'=8] {'core','z'}, dimensions={0} | all-to-all | bytes 196608 | tf_op jit(solution)/shard_map/all_to_all | solution.py:130
  114.7 0.6 reshape.23
  (4 shorter events, 0.1 us)
Async XLA Ops:
  0.0 24.0 %collective-permute-start = (bf16[48,48,2,768]{3,2,1,0:T(2,128)(2,1)}, bf16[48,48,2,768]{3,2,1,0:T(2,128)(2,1)}, u32[]{:S(2)}, u32[]{:S(2)}) collective-permute-start(bf16[48,48,2,768]{3,2,1,0:T(2,128)(2,1)} %param.3), channel_id=1, source_target_pairs={{0,16},{16,0},{1,17},{17,1},{2,18},{18,2},{3,19},{19,3},{4,20},{20... | collective-permute-start | bytes 21233672 | tf_op jit(solution)/shard_map/ppermute | solution.py:119
  8.8 62.0 %all-to-all-start = ((bf16[32,16,2304]{2,1,0:T(8,128)(2,1)}), bf16[32,16,2304]{2,1,0:T(8,128)(2,1)S(1)}, u32[]{:S(2)}, u32[]{:S(2)}) async-start(bf16[32,16,2304]{2,1,0:T(8,128)(2,1)} %pack.1), calls=%async_computation | async-start | bytes 4718592 | tf_op jit(solution)/shard_map/all_to_all | solution.py:121
  78.2 8.8 %collective-permute-start.1 = (f32[4,16,1536]{2,1,0:T(8,128)}, f32[4,16,1536]{2,1,0:T(8,128)S(1)}, u32[]{:S(2)}, u32[]{:S(2)}) collective-permute-start(f32[4,16,1536]{2,1,0:T(8,128)} %get-tuple-element.10), channel_id=1, source_target_pairs={{0,128},{16,48},{8,136},{24,56},{32,160},{48,16},{40,168},{56,24},... | collective-permute-start | bytes 1179656 | tf_op jit(solution)/shard_map/ppermute | solution.py:112
  80.8 9.2 %collective-permute-start.2 = (f32[4,16,1536]{2,1,0:T(8,128)S(1)}, f32[4,16,1536]{2,1,0:T(8,128)S(1)}, u32[]{:S(2)}, u32[]{:S(2)}) collective-permute-start(f32[4,16,1536]{2,1,0:T(8,128)S(1)} %get-tuple-element.11), channel_id=1, source_target_pairs={{0,64},{16,24},{8,72},{24,16},{32,96},{48,56},{40,104},{56,48},{64... | collective-permute-start | bytes 1179656 | tf_op jit(solution)/shard_map/ppermute | solution.py:112
  80.8 10.4 %collective-permute-start.3 = (f32[4,16,1536]{2,1,0:T(8,128)S(1)}, f32[4,16,1536]{2,1,0:T(8,128)S(1)}, u32[]{:S(2)}, u32[]{:S(2)}) collective-permute-start(f32[4,16,1536]{2,1,0:T(8,128)S(1)} %get-tuple-element.12), channel_id=1, source_target_pairs={{0,192},{16,56},{8,200},{24,48},{32,224},{48,24},{40,232},{56,16},... | collective-permute-start | bytes 1179656 | tf_op jit(solution)/shard_map/ppermute | solution.py:112
  91.3 5.1 %collective-permute-start.4 = (f32[16,1536]{1,0:T(8,128)S(1)}, f32[16,1536]{1,0:T(8,128)S(1)}, u32[]{:S(2)}, u32[]{:S(2)}) collective-permute-start(f32[16,1536]{1,0:T(8,128)S(1)} %get-tuple-element.13), channel_id=1, source_target_pairs={{0,32},{16,144},{8,40},{24,152},{32,0},{48,176},{40,8},{56,184},{6... | collective-permute-start | bytes 294920 | tf_op jit(solution)/shard_map/ppermute | solution.py:112
  94.0 4.0 %collective-permute-start.5 = (f32[16,1536]{1,0:T(8,128)S(1)}, f32[16,1536]{1,0:T(8,128)S(1)}, u32[]{:S(2)}, u32[]{:S(2)}) collective-permute-start(f32[16,1536]{1,0:T(8,128)S(1)} %get-tuple-element.15), channel_id=1, source_target_pairs={{0,8},{16,80},{8,0},{24,88},{32,40},{48,112},{40,32},{56,120},{64,... | collective-permute-start | bytes 294920 | tf_op jit(solution)/shard_map/ppermute | solution.py:112
  94.7 4.7 %collective-permute-start.6 = (f32[16,1536]{1,0:T(8,128)S(1)}, f32[16,1536]{1,0:T(8,128)S(1)}, u32[]{:S(2)}, u32[]{:S(2)}) collective-permute-start(f32[16,1536]{1,0:T(8,128)S(1)} %get-tuple-element.14), channel_id=1, source_target_pairs={{0,40},{16,208},{8,32},{24,216},{32,8},{48,240},{40,0},{56,248},{6... | collective-permute-start | bytes 294920 | tf_op jit(solution)/shard_map/ppermute | solution.py:112

commit v3 on v2

v3 whole, which is shorter than its diff:
```python
import itertools

import jax
import jax.numpy as jnp
from jax import lax
from jax.experimental import pallas as pl
from jax.experimental.pallas import tpu as pltpu
from jax.sharding import Mesh, PartitionSpec as P

AXES = ("y", "xh", "core", "xl", "z")
SIZES = (4, 2, 2, 2, 8)
MIB = 1024 * 1024


def pack_kernel(lam_ref, out_ref, taken, made, pick_ref, in_sems, out_sems):
    ins = [pltpu.make_async_copy(lam_ref.at[:, pl.ds(16 * m, 16)], taken.at[m], in_sems.at[m]) for m in range(3)]
    for copy in ins:
        copy.start()
    rows = lax.broadcasted_iota(jnp.int32, (512, 512), 0)
    cols = lax.broadcasted_iota(jnp.int32, (512, 512), 1)
    wanted = (2 * (rows % 16) + (rows // 16) % 2) * 16 + rows // 32
    pick_ref[...] = jnp.where(cols == wanted, 1.0, 0.0).astype(jnp.bfloat16)
    outs = []
    for m in range(3):
        ins[m].wait()
        y = jnp.dot(pick_ref[...], taken[m].reshape(512, 768), preferred_element_type=jnp.float32)
        y = y.astype(jnp.bfloat16).reshape(16, 2, 16, 768)
        for core in range(2):
            for j in range(16):
                made[m, core * 16 + j] = jnp.concatenate(
                    [y[c, core, :, 48 * j : 48 * j + 48] for c in range(16)], axis=-1
                )
        outs.append(pltpu.make_async_copy(made.at[m], out_ref.at[:, :, pl.ds(768 * m, 768)], out_sems.at[m]))
        outs[m].start()
    for copy in outs:
        copy.wait()


def pack(lam):
    return pl.pallas_call(
        pack_kernel,
        in_specs=[pl.BlockSpec(memory_space=pl.ANY)],
        out_specs=pl.BlockSpec(memory_space=pl.ANY),
        out_shape=jax.ShapeDtypeStruct((32, 16, 2304), jnp.bfloat16),
        scratch_shapes=[
            pltpu.VMEM((3, 32, 16, 768), jnp.bfloat16),
            pltpu.VMEM((3, 32, 16, 768), jnp.bfloat16),
            pltpu.VMEM((512, 512), jnp.bfloat16),
            pltpu.SemaphoreType.DMA((3,)),
            pltpu.SemaphoreType.DMA((3,)),
        ],
        compiler_params=pltpu.CompilerParams(vmem_limit_bytes=60 * MIB),
        cost_estimate=pl.CostEstimate(flops=3 * 2 * 512 * 512 * 768, bytes_accessed=4 * 1179648, transcendentals=0),
        name="pack",
    )(lam)


DEPTH = 256
STEPS = 2304 // DEPTH


def product_kernel(at_ref, x_ref, w_own_ref, w_oth_ref, *rest):
    outs, (held, acc_ref, sems) = rest[:4], rest[4:]
    copies = []
    for s, w in enumerate((w_own_ref, w_oth_ref)):
        for k in range(STEPS):
            copies.append(pltpu.make_async_copy(w.at[pl.ds(k * DEPTH, DEPTH)], held.at[s, k], sems.at[s, k]))
            copies[-1].start()
    core, y, x_at = at_ref[0], at_ref[1], at_ref[2]
    blocks = [(y ^ (p // 4)) * 4 + ((x_at // 2) ^ (p // 2 % 2)) * 2 + p % 2 for p in range(16)]
    swap = x_at % 2 == 1

    def term(s, k, n):
        x = x_ref.at[core if s == 0 else 1 - core]
        lhs = jnp.concatenate([x[block, :, k * DEPTH : (k + 1) * DEPTH] for block in blocks], axis=0)
        return jnp.dot(lhs, held[s, k, :, n : n + 512], preferred_element_type=jnp.float32)

    for s in range(2):
        for k in range(STEPS):
            copies[s * STEPS + k].wait()
            if (s, k) == (1, STEPS - 1):
                break
            for n in range(0, 1536, 512):
                if s + k == 0:
                    acc_ref[:, n : n + 512] = term(s, k, n)
                else:
                    acc_ref[:, n : n + 512] += term(s, k, n)

    def total(n):
        return (0.5 * (acc_ref[:, n : n + 512] + term(1, STEPS - 1, n))).reshape(16, 2, 8, 512)

    for first in range(2):

        @pl.when(core == first)
        def _():
            for n in range(0, 1536, 512):
                done = total(n)
                for (flip, out_ref), late, c in itertools.product(enumerate(outs), range(4), range(2)):
                    flip_y, flip_x = (flip, late) if first == 0 else (late, flip)
                    rows = done[(flip_y * 2 + flip_x // 2) * 2 + c]
                    low, high = rows[flip_x % 2], rows[1 - flip_x % 2]
                    out_ref[late, 8 * c : 8 * c + 8, n : n + 512] = jnp.where(swap, high, low)


def product(at, received, w_own, w_oth):
    in_hbm = [pltpu.with_memory_space_constraint(w, pltpu.HBM) for w in (w_own, w_oth)]
    return pl.pallas_call(
        product_kernel,
        in_specs=[
            pl.BlockSpec(memory_space=pltpu.SMEM),
            pl.BlockSpec(memory_space=pltpu.VMEM),
            pl.BlockSpec(memory_space=pl.ANY),
            pl.BlockSpec(memory_space=pl.ANY),
        ],
        out_specs=[pl.BlockSpec(memory_space=pltpu.VMEM)] * 4,
        out_shape=[pltpu.VMEM((4, 16, 1536), jnp.float32)] * 4,
        scratch_shapes=[
            pltpu.VMEM((2, STEPS, DEPTH, 1536), jnp.bfloat16),
            pltpu.VMEM((256, 1536), jnp.float32),
            pltpu.SemaphoreType.DMA((2, STEPS)),
        ],
        compiler_params=pltpu.CompilerParams(vmem_limit_bytes=20 * MIB),
        cost_estimate=pl.CostEstimate(flops=2 * 256 * 4608 * 1536, bytes_accessed=18 * MIB, transcendentals=0),
        name="product",
    )(at, received.reshape(2, 16, 16, 2304), *in_hbm)


def pairs(flip, first):
    out = []
    for y, x, core in itertools.product(range(4), range(4), range(2)):
        to_y, to_x = (y ^ flip, x) if core == first else (y, x ^ flip)
        out.append(tuple(((b * 2 + a // 2) * 2 + core) * 2 + a % 2 for b, a in ((y, x), (to_y, to_x))))
    return out


def moved(piece, flip, first):
    return lax.ppermute(piece, ("y", "xh", "core", "xl"), pairs(flip, first))


def shards(lam, ints):
    core = lax.axis_index("core").astype(jnp.int32)
    y, x = lax.axis_index("y").astype(jnp.int32), lax.axis_index(("xh", "xl")).astype(jnp.int32)
    ints_oth = lax.ppermute(ints, "core", [(0, 1), (1, 0)])
    w_own, w_oth = ints.reshape(2304, 1536), ints_oth.reshape(2304, 1536)
    received = lax.all_to_all(pack(lam), ("core", "xl", "z"), 0, 0)
    part = product(jnp.stack([core, y, x]), received, w_own, w_oth)
    total = part[0]
    for flip in (2, 1, 3):
        total = total + moved(part[flip], flip, 0)
    pieces = [total[flip] for flip in range(4)]
    total = pieces[0]
    for flip in (2, 1, 3):
        total = total + moved(pieces[flip], flip, 1)
    total = lax.all_to_all(total.reshape(16, 12, 128), ("core", "z"), 0, 0)
    return total.reshape(2, 8, 12, 128).sum(1).reshape(2, 2, 768)


def solution(mesh):
    fine = Mesh(mesh.devices.reshape(SIZES), AXES)
    wide, blk = AXES[:3], AXES[3:]
    in_specs = (P(blk, wide, None), P(wide, blk, None, None))
    out_specs = P(AXES, None, None)
    return jax.shard_map(shards, mesh=fine, in_specs=in_specs, out_specs=out_specs, check_vma=False)
```

time: 116 us -> 114 us (0.983)
  Pallas kernels: 13 us -> 11.6 us
  transfers between devices with their start and end apart: 8 -> 8, of which waited for: 7 -> 7; matrix products, arithmetic and copies ran while one was open for 12% -> 13% of each run, Pallas kernels for 5% -> 4%
where the time goes in v3:
time: 114 us
  waiting for transfers between devices  53.7 us (47%)
  starting transfers between devices  18 us (16%)
  blocking collectives  15.2 us (13%)
  local copies, waits for them, and re-layouts  14.9 us (13%)
  Pallas kernels  11.6 us (10%)
    all_to_all x1, waiting for transfers between devices, shards(): received = lax.all_to_all(pack(lam), ('core', 'xl', 'z'), 0, 0)  39.8 us
    all_to_all x1, blocking collectives, shards(): total = lax.all_to_all(total.reshape(16, 12, 128), ('core', 'z'), 0, 0)  15.2 us
    unnamed x2, local copies, waits for them, and re-layouts  14.2 us
    ppermute x6, waiting for transfers between devices, moved(): return lax.ppermute(piece, ('y', 'xh', 'core', 'xl'), pairs(flip, first))  14 us
    all_to_all x1, starting transfers between devices, shards(): received = lax.all_to_all(pack(lam), ('core', 'xl', 'z'), 0, 0)  7.94 us
    ppermute x6, starting transfers between devices, moved(): return lax.ppermute(piece, ('y', 'xh', 'core', 'xl'), pairs(flip, first))  6.82 us
    pallas_call x1, Pallas kernels, product(): pl.pallas_call(product_kernel, in_specs=[pl.BlockSpec(memory_space=pltpu....  6.65 us
    pallas_call x1, Pallas kernels, pack(): pl.pallas_call(pack_kernel, in_specs=[pl.BlockSpec(memory_space=pl.ANY)],...  4.99 us
  transfers between devices with their start and end apart: 8, of which 7 were waited for; matrix products, arithmetic and copies ran while one was open for 13% of the time, Pallas kernels for 4%

profile of v3, /device:TPU:1, one launch (start us, length us, event | category | flops | bytes accessed | tf_op | source)
XLA Modules:
  0.0 113.8 jit_solution(13886946126685420362)
XLA Ops:
  0.0 3.2 %collective-permute-start = (bf16[48,48,2,768]{3,2,1,0:T(2,128)(2,1)}, bf16[48,48,2,768]{3,2,1,0:T(2,128)(2,1)}, u32[]{:S(2)}, u32[]{:S(2)}) collective-permute-start(bf16[48,48,2,768]{3,2,1,0:T(2,128)(2,1)} %param.3), channel_id=1, source_target_pairs={{0,16},{16,0},{1,17},{17,1},{2,18},{18,2},{3,19},{19,3},{4,20},{20... | collective-permute-start | bytes 21233672 | tf_op jit(solution)/shard_map/ppermute | solution.py:143
  3.2 5.0 %pack.1 = bf16[32,16,2304]{2,1,0:T(8,128)(2,1)} custom-call(bf16[32,48,768]{2,1,0:T(8,128)(2,1)} %lam_ref.1), custom_call_target="tpu_custom_call" | custom-call | flops 1207959552 | bytes 4718592 | tf_op jit(solution)/shard_map/pack/pallas_call | solution.py:40
  8.2 7.9 %all-to-all-start = ((bf16[32,16,2304]{2,1,0:T(8,128)(2,1)}), bf16[32,16,2304]{2,1,0:T(8,128)(2,1)S(1)}, u32[]{:S(2)}, u32[]{:S(2)}) async-start(bf16[32,16,2304]{2,1,0:T(8,128)(2,1)} %pack.1), calls=%async_computation | async-start | bytes 4718592 | tf_op jit(solution)/shard_map/all_to_all | solution.py:145
  16.2 7.2 %copy.3 = bf16[288,8,2,768]{3,1,2,0:T(8,128)(2,1)} copy(bf16[288,8,2,768]{3,2,1,0:T(2,128)(2,1)} %bitcast.29) | data formatting | bytes 14155776
  23.4 0.1 pad_add_fusion.at_ref
  23.5 0.0 collective-permute-done
  23.5 7.1 %copy.4 = bf16[288,8,2,768]{3,1,2,0:T(8,128)(2,1)} copy(bf16[288,8,2,768]{3,2,1,0:T(2,128)(2,1)} %bitcast.13) | data formatting | bytes 14155776
  30.5 39.8 %all-to-all-done = bf16[32,16,2304]{2,1,0:T(8,128)(2,1)S(1)} async-done(((bf16[32,16,2304]{2,1,0:T(8,128)(2,1)}), bf16[32,16,2304]{2,1,0:T(8,128)(2,1)S(1)}, u32[]{:S(2)}, u32[]{:S(2)}) %all-to-all-start) | async-done | bytes 2359328 | tf_op jit(solution)/shard_map/all_to_all | solution.py:145
  70.3 6.7 %product.1 = (f32[4,16,1536]{2,1,0:T(8,128)S(1)}, f32[4,16,1536]{2,1,0:T(8,128)S(1)}, f32[4,16,1536]{2,1,0:T(8,128)S(1)}, f32[4,16,1536]{2,1,0:T(8,128)S(1)}) custom-call(s32[3]{0:T(128)S(1)} %pad_add_fusion.at_ref, bf16[2,16,16,2304]{3,2,1,0:T(8,128)(2,1)S(1)} %bitcast.26, bf16[2304,1536]{1,0:T(8,128)(2,1)} %bitcast.27, bf16[2304,1536]{1,0:T(8,128)(2,1)} %bitcast.28), custom_call_target="tpu_custom_call" | custom-call | flops 3623878656 | bytes 18874368 | tf_op jit(solution)/shard_map/product/pallas_call | solution.py:107
  76.9 2.5 %collective-permute-start.1 = (f32[4,16,1536]{2,1,0:T(8,128)S(1)}, f32[4,16,1536]{2,1,0:T(8,128)S(1)}, u32[]{:S(2)}, u32[]{:S(2)}) collective-permute-start(f32[4,16,1536]{2,1,0:T(8,128)S(1)} %get-tuple-element.10), channel_id=1, source_target_pairs={{0,128},{16,48},{8,136},{24,56},{32,160},{48,16},{40,168},{56,24},... | collective-permute-start | bytes 1179656 | tf_op jit(solution)/shard_map/ppermute | solution.py:137
  79.5 0.0 collective-permute-start.2
  79.5 0.8 collective-permute-start.3
  80.3 5.2 %collective-permute-done.1 = f32[4,16,1536]{2,1,0:T(8,128)S(1)} collective-permute-done((f32[4,16,1536]{2,1,0:T(8,128)S(1)}, f32[4,16,1536]{2,1,0:T(8,128)S(1)}, u32[]{:S(2)}, u32[]{:S(2)}) %collective-permute-start.1) | collective-permute-done | bytes 393248 | tf_op jit(solution)/shard_map/ppermute | solution.py:137
  85.5 3.0 %collective-permute-done.2 = f32[4,16,1536]{2,1,0:T(8,128)S(1)} collective-permute-done((f32[4,16,1536]{2,1,0:T(8,128)S(1)}, f32[4,16,1536]{2,1,0:T(8,128)S(1)}, u32[]{:S(2)}, u32[]{:S(2)}) %collective-permute-start.2) | collective-permute-done | bytes 393248 | tf_op jit(solution)/shard_map/ppermute | solution.py:137
  88.4 1.2 %collective-permute-done.3 = f32[4,16,1536]{2,1,0:T(8,128)S(1)} collective-permute-done((f32[4,16,1536]{2,1,0:T(8,128)S(1)}, f32[4,16,1536]{2,1,0:T(8,128)S(1)}, u32[]{:S(2)}, u32[]{:S(2)}) %collective-permute-start.3) | collective-permute-done | bytes 393248 | tf_op jit(solution)/shard_map/ppermute | solution.py:137
  89.7 0.1 add_add_fusion
  89.8 2.7 %collective-permute-start.4 = (f32[16,1536]{1,0:T(8,128)S(1)}, f32[16,1536]{1,0:T(8,128)S(1)}, u32[]{:S(2)}, u32[]{:S(2)}) collective-permute-start(f32[16,1536]{1,0:T(8,128)S(1)} %get-tuple-element.13), channel_id=1, source_target_pairs={{0,32},{16,144},{8,40},{24,152},{32,0},{48,176},{40,8},{56,184},{6... | collective-permute-start | bytes 294920 | tf_op jit(solution)/shard_map/ppermute | solution.py:137
  92.5 0.7 collective-permute-start.5
  93.2 0.1 collective-permute-start.6
  93.2 1.6 %collective-permute-done.4 = f32[16,1536]{1,0:T(8,128)S(1)} collective-permute-done((f32[16,1536]{1,0:T(8,128)S(1)}, f32[16,1536]{1,0:T(8,128)S(1)}, u32[]{:S(2)}, u32[]{:S(2)}) %collective-permute-start.4) | collective-permute-done | bytes 98336 | tf_op jit(solution)/shard_map/ppermute | solution.py:137
  94.8 1.7 %collective-permute-done.5 = f32[16,1536]{1,0:T(8,128)S(1)} collective-permute-done((f32[16,1536]{1,0:T(8,128)S(1)}, f32[16,1536]{1,0:T(8,128)S(1)}, u32[]{:S(2)}, u32[]{:S(2)}) %collective-permute-start.5) | collective-permute-done | bytes 98336 | tf_op jit(solution)/shard_map/ppermute | solution.py:137
  96.5 1.3 %collective-permute-done.6 = f32[16,1536]{1,0:T(8,128)S(1)} collective-permute-done((f32[16,1536]{1,0:T(8,128)S(1)}, f32[16,1536]{1,0:T(8,128)S(1)}, u32[]{:S(2)}, u32[]{:S(2)}) %collective-permute-start.6) | collective-permute-done | bytes 98336 | tf_op jit(solution)/shard_map/ppermute | solution.py:137
  97.9 15.2 %all_to_all.10 = f32[16,12,128]{2,1,0:T(8,128)S(1)} all-to-all(f32[16,12,128]{2,1,0:T(8,128)S(1)} %reshape.21), channel_id=1, replica_groups=mesh['y'=4,'xh'=2,'core'=2,'xl'=2,'z'=8] {'core','z'}, dimensions={0} | all-to-all | bytes 196608 | tf_op jit(solution)/shard_map/all_to_all | solution.py:154
  113.2 0.6 reshape.23
  (4 shorter events, 0.1 us)
Async XLA Ops:
  0.0 23.5 %collective-permute-start = (bf16[48,48,2,768]{3,2,1,0:T(2,128)(2,1)}, bf16[48,48,2,768]{3,2,1,0:T(2,128)(2,1)}, u32[]{:S(2)}, u32[]{:S(2)}) collective-permute-start(bf16[48,48,2,768]{3,2,1,0:T(2,128)(2,1)} %param.3), channel_id=1, source_target_pairs={{0,16},{16,0},{1,17},{17,1},{2,18},{18,2},{3,19},{19,3},{4,20},{20... | collective-permute-start | bytes 21233672 | tf_op jit(solution)/shard_map/ppermute | solution.py:143
  8.2 62.0 %all-to-all-start = ((bf16[32,16,2304]{2,1,0:T(8,128)(2,1)}), bf16[32,16,2304]{2,1,0:T(8,128)(2,1)S(1)}, u32[]{:S(2)}, u32[]{:S(2)}) async-start(bf16[32,16,2304]{2,1,0:T(8,128)(2,1)} %pack.1), calls=%async_computation | async-start | bytes 4718592 | tf_op jit(solution)/shard_map/all_to_all | solution.py:145
  76.9 8.6 %collective-permute-start.1 = (f32[4,16,1536]{2,1,0:T(8,128)S(1)}, f32[4,16,1536]{2,1,0:T(8,128)S(1)}, u32[]{:S(2)}, u32[]{:S(2)}) collective-permute-start(f32[4,16,1536]{2,1,0:T(8,128)S(1)} %get-tuple-element.10), channel_id=1, source_target_pairs={{0,128},{16,48},{8,136},{24,56},{32,160},{48,16},{40,168},{56,24},... | collective-permute-start | bytes 1179656 | tf_op jit(solution)/shard_map/ppermute | solution.py:137
  79.5 9.0 %collective-permute-start.2 = (f32[4,16,1536]{2,1,0:T(8,128)S(1)}, f32[4,16,1536]{2,1,0:T(8,128)S(1)}, u32[]{:S(2)}, u32[]{:S(2)}) collective-permute-start(f32[4,16,1536]{2,1,0:T(8,128)S(1)} %get-tuple-element.11), channel_id=1, source_target_pairs={{0,64},{16,24},{8,72},{24,16},{32,96},{48,56},{40,104},{56,48},{64... | collective-permute-start | bytes 1179656 | tf_op jit(solution)/shard_map/ppermute | solution.py:137
  79.5 10.2 %collective-permute-start.3 = (f32[4,16,1536]{2,1,0:T(8,128)S(1)}, f32[4,16,1536]{2,1,0:T(8,128)S(1)}, u32[]{:S(2)}, u32[]{:S(2)}) collective-permute-start(f32[4,16,1536]{2,1,0:T(8,128)S(1)} %get-tuple-element.12), channel_id=1, source_target_pairs={{0,192},{16,56},{8,200},{24,48},{32,224},{48,24},{40,232},{56,16},... | collective-permute-start | bytes 1179656 | tf_op jit(solution)/shard_map/ppermute | solution.py:137
  89.8 5.1 %collective-permute-start.4 = (f32[16,1536]{1,0:T(8,128)S(1)}, f32[16,1536]{1,0:T(8,128)S(1)}, u32[]{:S(2)}, u32[]{:S(2)}) collective-permute-start(f32[16,1536]{1,0:T(8,128)S(1)} %get-tuple-element.13), channel_id=1, source_target_pairs={{0,32},{16,144},{8,40},{24,152},{32,0},{48,176},{40,8},{56,184},{6... | collective-permute-start | bytes 294920 | tf_op jit(solution)/shard_map/ppermute | solution.py:137
  92.5 4.0 %collective-permute-start.5 = (f32[16,1536]{1,0:T(8,128)S(1)}, f32[16,1536]{1,0:T(8,128)S(1)}, u32[]{:S(2)}, u32[]{:S(2)}) collective-permute-start(f32[16,1536]{1,0:T(8,128)S(1)} %get-tuple-element.15), channel_id=1, source_target_pairs={{0,8},{16,80},{8,0},{24,88},{32,40},{48,112},{40,32},{56,120},{64,... | collective-permute-start | bytes 294920 | tf_op jit(solution)/shard_map/ppermute | solution.py:137
  93.2 4.7 %collective-permute-start.6 = (f32[16,1536]{1,0:T(8,128)S(1)}, f32[16,1536]{1,0:T(8,128)S(1)}, u32[]{:S(2)}, u32[]{:S(2)}) collective-permute-start(f32[16,1536]{1,0:T(8,128)S(1)} %get-tuple-element.14), channel_id=1, source_target_pairs={{0,40},{16,208},{8,32},{24,216},{32,8},{48,240},{40,0},{56,248},{6... | collective-permute-start | bytes 294920 | tf_op jit(solution)/shard_map/ppermute | solution.py:137

commit v4 on v3

--- a/solution.py
+++ b/solution.py
@@ -16,19 +16,23 @@
     ins = [pltpu.make_async_copy(lam_ref.at[:, pl.ds(16 * m, 16)], taken.at[m], in_sems.at[m]) for m in range(3)]
     for copy in ins:
         copy.start()
-    rows = lax.broadcasted_iota(jnp.int32, (512, 512), 0)
-    cols = lax.broadcasted_iota(jnp.int32, (512, 512), 1)
-    wanted = (2 * (rows % 16) + (rows // 16) % 2) * 16 + rows // 32
+    rows = lax.broadcasted_iota(jnp.int32, (256, 256), 0)
+    cols = lax.broadcasted_iota(jnp.int32, (256, 256), 1)
+    wanted = (2 * (rows % 8) + (rows // 8) % 2) * 16 + rows // 16
     pick_ref[...] = jnp.where(cols == wanted, 1.0, 0.0).astype(jnp.bfloat16)
     outs = []
     for m in range(3):
         ins[m].wait()
-        y = jnp.dot(pick_ref[...], taken[m].reshape(512, 768), preferred_element_type=jnp.float32)
-        y = y.astype(jnp.bfloat16).reshape(16, 2, 16, 768)
+        halves = [
+            jnp.dot(pick_ref[...], taken[m, 16 * h : 16 * h + 16].reshape(256, 768), preferred_element_type=jnp.float32)
+            for h in range(2)
+        ]
+        halves = [half.reshape(16, 2, 8, 768) for half in halves]
         for core in range(2):
+            y = jnp.concatenate([half[:, core] for half in halves], axis=1).astype(jnp.bfloat16)
             for j in range(16):
                 made[m, core * 16 + j] = jnp.concatenate(
-                    [y[c, core, :, 48 * j : 48 * j + 48] for c in range(16)], axis=-1
+                    [y[c, :, 48 * j : 48 * j + 48] for c in range(16)], axis=-1
                 )
         outs.append(pltpu.make_async_copy(made.at[m], out_ref.at[:, :, pl.ds(768 * m, 768)], out_sems.at[m]))
         outs[m].start()
@@ -45,12 +49,12 @@
         scratch_shapes=[
             pltpu.VMEM((3, 32, 16, 768), jnp.bfloat16),
             pltpu.VMEM((3, 32, 16, 768), jnp.bfloat16),
-            pltpu.VMEM((512, 512), jnp.bfloat16),
+            pltpu.VMEM((256, 256), jnp.bfloat16),
             pltpu.SemaphoreType.DMA((3,)),
             pltpu.SemaphoreType.DMA((3,)),
         ],
         compiler_params=pltpu.CompilerParams(vmem_limit_bytes=60 * MIB),
-        cost_estimate=pl.CostEstimate(flops=3 * 2 * 512 * 512 * 768, bytes_accessed=4 * 1179648, transcendentals=0),
+        cost_estimate=pl.CostEstimate(flops=3 * 4 * 256 * 256 * 768, bytes_accessed=4 * 1179648, transcendentals=0),
         name="pack",
     )(lam)
 
@@ -140,9 +144,10 @@
 def shards(lam, ints):
     core = lax.axis_index("core").astype(jnp.int32)
     y, x = lax.axis_index("y").astype(jnp.int32), lax.axis_index(("xh", "xl")).astype(jnp.int32)
+    ints, sent = lax.optimization_barrier((ints, pack(lam)))
     ints_oth = lax.ppermute(ints, "core", [(0, 1), (1, 0)])
     w_own, w_oth = ints.reshape(2304, 1536), ints_oth.reshape(2304, 1536)
-    received = lax.all_to_all(pack(lam), ("core", "xl", "z"), 0, 0)
+    received = lax.all_to_all(sent, ("core", "xl", "z"), 0, 0)
     part = product(jnp.stack([core, y, x]), received, w_own, w_oth)
     total = part[0]
     for flip in (2, 1, 3):
@@ -151,8 +156,8 @@
     total = pieces[0]
     for flip in (2, 1, 3):
         total = total + moved(pieces[flip], flip, 1)
-    total = lax.all_to_all(total.reshape(16, 12, 128), ("core", "z"), 0, 0)
-    return total.reshape(2, 8, 12, 128).sum(1).reshape(2, 2, 768)
+    total = lax.all_to_all(total.reshape(16, 2, 768), ("core", "z"), 0, 0)
+    return total.reshape(2, 8, 2, 768).sum(1)
 
 
 def solution(mesh):

time: 114 us -> 114 us (level)
  transfers between devices with their start and end apart: 8 -> 8, of which waited for: 7 -> 7; matrix products, arithmetic and copies ran while one was open for 13% -> 13% of each run, Pallas kernels for 4% -> 0%
where the time goes in v4:
time: 114 us
  waiting for transfers between devices  53.7 us (47%)
  starting transfers between devices  18.1 us (16%)
  blocking collectives  15.3 us (13%)
  local copies, waits for them, and re-layouts  14.3 us (13%)
  Pallas kernels  11.5 us (10%)
    all_to_all x1, waiting for transfers between devices, shards(): received = lax.all_to_all(sent, ('core', 'xl', 'z'), 0, 0)  39.8 us
    all_to_all x1, blocking collectives, shards(): total = lax.all_to_all(total.reshape(16, 2, 768), ('core', 'z'), 0, 0)  15.3 us
    unnamed x2, local copies, waits for them, and re-layouts  14.2 us
    ppermute x6, waiting for transfers between devices, moved(): return lax.ppermute(piece, ('y', 'xh', 'core', 'xl'), pairs(flip, first))  14 us
    all_to_all x1, starting transfers between devices, shards(): received = lax.all_to_all(sent, ('core', 'xl', 'z'), 0, 0)  7.93 us
    ppermute x6, starting transfers between devices, moved(): return lax.ppermute(piece, ('y', 'xh', 'core', 'xl'), pairs(flip, first))  6.82 us
    pallas_call x1, Pallas kernels, product(): pl.pallas_call(product_kernel, in_specs=[pl.BlockSpec(memory_space=pltpu....  6.65 us
    pallas_call x1, Pallas kernels, pack(): pl.pallas_call(pack_kernel, in_specs=[pl.BlockSpec(memory_space=pl.ANY)],...  4.81 us
  transfers between devices with their start and end apart: 8, of which 7 were waited for; matrix products, arithmetic and copies ran while one was open for 13% of the time, Pallas kernels for 0%

profile of v4, /device:TPU:1, one launch (start us, length us, event | category | flops | bytes accessed | tf_op | source)
XLA Modules:
  0.0 113.8 jit_solution(12735602546870386216)
XLA Ops:
  0.0 4.8 %pack.1 = bf16[32,16,2304]{2,1,0:T(8,128)(2,1)} custom-call(bf16[32,48,768]{2,1,0:T(8,128)(2,1)} %lam_ref.1), custom_call_target="tpu_custom_call" | custom-call | flops 603979776 | bytes 4718592 | tf_op jit(solution)/shard_map/pack/pallas_call | solution.py:44
  4.8 3.3 %collective-permute-start = (bf16[48,48,2,768]{3,2,1,0:T(2,128)(2,1)}, bf16[48,48,2,768]{3,2,1,0:T(2,128)(2,1)}, u32[]{:S(2)}, u32[]{:S(2)}) collective-permute-start(bf16[48,48,2,768]{3,2,1,0:T(2,128)(2,1)} %param.3), channel_id=1, source_target_pairs={{0,16},{16,0},{1,17},{17,1},{2,18},{18,2},{3,19},{19,3},{4,20},{20... | collective-permute-start | bytes 21233672 | tf_op jit(solution)/shard_map/ppermute | solution.py:148
  8.1 7.9 %all-to-all-start = ((bf16[32,16,2304]{2,1,0:T(8,128)(2,1)}), bf16[32,16,2304]{2,1,0:T(8,128)(2,1)S(1)}, u32[]{:S(2)}, u32[]{:S(2)}) async-start(bf16[32,16,2304]{2,1,0:T(8,128)(2,1)} %pack.1), calls=%async_computation | async-start | bytes 4718592 | tf_op jit(solution)/shard_map/all_to_all | solution.py:150
  16.1 7.2 %copy.3 = bf16[288,8,2,768]{3,1,2,0:T(8,128)(2,1)} copy(bf16[288,8,2,768]{3,2,1,0:T(2,128)(2,1)} %bitcast.29) | data formatting | bytes 14155776
  23.3 0.1 pad_add_fusion.at_ref
  23.3 0.0 collective-permute-done
  23.4 7.1 %copy.4 = bf16[288,8,2,768]{3,1,2,0:T(8,128)(2,1)} copy(bf16[288,8,2,768]{3,2,1,0:T(2,128)(2,1)} %bitcast.13) | data formatting | bytes 14155776
  30.4 39.8 %all-to-all-done = bf16[32,16,2304]{2,1,0:T(8,128)(2,1)S(1)} async-done(((bf16[32,16,2304]{2,1,0:T(8,128)(2,1)}), bf16[32,16,2304]{2,1,0:T(8,128)(2,1)S(1)}, u32[]{:S(2)}, u32[]{:S(2)}) %all-to-all-start) | async-done | bytes 2359328 | tf_op jit(solution)/shard_map/all_to_all | solution.py:150
  70.2 6.7 %product.1 = (f32[4,16,1536]{2,1,0:T(8,128)S(1)}, f32[4,16,1536]{2,1,0:T(8,128)S(1)}, f32[4,16,1536]{2,1,0:T(8,128)S(1)}, f32[4,16,1536]{2,1,0:T(8,128)S(1)}) custom-call(s32[3]{0:T(128)S(1)} %pad_add_fusion.at_ref, bf16[2,16,16,2304]{3,2,1,0:T(8,128)(2,1)S(1)} %bitcast.26, bf16[2304,1536]{1,0:T(8,128)(2,1)} %bitcast.27, bf16[2304,1536]{1,0:T(8,128)(2,1)} %bitcast.28), custom_call_target="tpu_custom_call" | custom-call | flops 3623878656 | bytes 18874368 | tf_op jit(solution)/shard_map/product/pallas_call | solution.py:111
  76.8 2.5 %collective-permute-start.1 = (f32[4,16,1536]{2,1,0:T(8,128)S(1)}, f32[4,16,1536]{2,1,0:T(8,128)S(1)}, u32[]{:S(2)}, u32[]{:S(2)}) collective-permute-start(f32[4,16,1536]{2,1,0:T(8,128)S(1)} %get-tuple-element.14), channel_id=1, source_target_pairs={{0,128},{16,48},{8,136},{24,56},{32,160},{48,16},{40,168},{56,24},... | collective-permute-start | bytes 1179656 | tf_op jit(solution)/shard_map/ppermute | solution.py:141
  79.4 0.0 collective-permute-start.2
  79.4 0.8 collective-permute-start.3
  80.2 5.2 %collective-permute-done.1 = f32[4,16,1536]{2,1,0:T(8,128)S(1)} collective-permute-done((f32[4,16,1536]{2,1,0:T(8,128)S(1)}, f32[4,16,1536]{2,1,0:T(8,128)S(1)}, u32[]{:S(2)}, u32[]{:S(2)}) %collective-permute-start.1) | collective-permute-done | bytes 393248 | tf_op jit(solution)/shard_map/ppermute | solution.py:141
  85.4 3.0 %collective-permute-done.2 = f32[4,16,1536]{2,1,0:T(8,128)S(1)} collective-permute-done((f32[4,16,1536]{2,1,0:T(8,128)S(1)}, f32[4,16,1536]{2,1,0:T(8,128)S(1)}, u32[]{:S(2)}, u32[]{:S(2)}) %collective-permute-start.2) | collective-permute-done | bytes 393248 | tf_op jit(solution)/shard_map/ppermute | solution.py:141
  88.3 1.2 %collective-permute-done.3 = f32[4,16,1536]{2,1,0:T(8,128)S(1)} collective-permute-done((f32[4,16,1536]{2,1,0:T(8,128)S(1)}, f32[4,16,1536]{2,1,0:T(8,128)S(1)}, u32[]{:S(2)}, u32[]{:S(2)}) %collective-permute-start.3) | collective-permute-done | bytes 393248 | tf_op jit(solution)/shard_map/ppermute | solution.py:141
  89.5 0.1 add_add_fusion
  89.7 2.7 %collective-permute-start.4 = (f32[16,1536]{1,0:T(8,128)S(1)}, f32[16,1536]{1,0:T(8,128)S(1)}, u32[]{:S(2)}, u32[]{:S(2)}) collective-permute-start(f32[16,1536]{1,0:T(8,128)S(1)} %get-tuple-element.17), channel_id=1, source_target_pairs={{0,32},{16,144},{8,40},{24,152},{32,0},{48,176},{40,8},{56,184},{6... | collective-permute-start | bytes 294920 | tf_op jit(solution)/shard_map/ppermute | solution.py:141
  92.4 0.7 collective-permute-start.5
  93.1 0.1 collective-permute-start.6
  93.1 1.6 %collective-permute-done.4 = f32[16,1536]{1,0:T(8,128)S(1)} collective-permute-done((f32[16,1536]{1,0:T(8,128)S(1)}, f32[16,1536]{1,0:T(8,128)S(1)}, u32[]{:S(2)}, u32[]{:S(2)}) %collective-permute-start.4) | collective-permute-done | bytes 98336 | tf_op jit(solution)/shard_map/ppermute | solution.py:141
  94.7 1.7 %collective-permute-done.5 = f32[16,1536]{1,0:T(8,128)S(1)} collective-permute-done((f32[16,1536]{1,0:T(8,128)S(1)}, f32[16,1536]{1,0:T(8,128)S(1)}, u32[]{:S(2)}, u32[]{:S(2)}) %collective-permute-start.5) | collective-permute-done | bytes 98336 | tf_op jit(solution)/shard_map/ppermute | solution.py:141
  96.4 1.3 %collective-permute-done.6 = f32[16,1536]{1,0:T(8,128)S(1)} collective-permute-done((f32[16,1536]{1,0:T(8,128)S(1)}, f32[16,1536]{1,0:T(8,128)S(1)}, u32[]{:S(2)}, u32[]{:S(2)}) %collective-permute-start.6) | collective-permute-done | bytes 98336 | tf_op jit(solution)/shard_map/ppermute | solution.py:141
  97.8 0.1 reshape.18
  97.8 15.3 %all_to_all.10 = f32[16,2,768]{2,1,0:T(2,128)S(1)} all-to-all(f32[16,2,768]{2,1,0:T(2,128)S(1)} %reshape.18), channel_id=1, replica_groups=mesh['y'=4,'xh'=2,'core'=2,'xl'=2,'z'=8] {'core','z'}, dimensions={0} | all-to-all | bytes 196608 | tf_op jit(solution)/shard_map/all_to_all | solution.py:159
  113.2 0.6 bitcast_reduce_fusion
  (2 shorter events, 0.1 us)
Async XLA Ops:
  4.8 18.5 %collective-permute-start = (bf16[48,48,2,768]{3,2,1,0:T(2,128)(2,1)}, bf16[48,48,2,768]{3,2,1,0:T(2,128)(2,1)}, u32[]{:S(2)}, u32[]{:S(2)}) collective-permute-start(bf16[48,48,2,768]{3,2,1,0:T(2,128)(2,1)} %param.3), channel_id=1, source_target_pairs={{0,16},{16,0},{1,17},{17,1},{2,18},{18,2},{3,19},{19,3},{4,20},{20... | collective-permute-start | bytes 21233672 | tf_op jit(solution)/shard_map/ppermute | solution.py:148
  8.1 62.0 %all-to-all-start = ((bf16[32,16,2304]{2,1,0:T(8,128)(2,1)}), bf16[32,16,2304]{2,1,0:T(8,128)(2,1)S(1)}, u32[]{:S(2)}, u32[]{:S(2)}) async-start(bf16[32,16,2304]{2,1,0:T(8,128)(2,1)} %pack.1), calls=%async_computation | async-start | bytes 4718592 | tf_op jit(solution)/shard_map/all_to_all | solution.py:150
  76.8 8.6 %collective-permute-start.1 = (f32[4,16,1536]{2,1,0:T(8,128)S(1)}, f32[4,16,1536]{2,1,0:T(8,128)S(1)}, u32[]{:S(2)}, u32[]{:S(2)}) collective-permute-start(f32[4,16,1536]{2,1,0:T(8,128)S(1)} %get-tuple-element.14), channel_id=1, source_target_pairs={{0,128},{16,48},{8,136},{24,56},{32,160},{48,16},{40,168},{56,24},... | collective-permute-start | bytes 1179656 | tf_op jit(solution)/shard_map/ppermute | solution.py:141
  79.4 9.0 %collective-permute-start.2 = (f32[4,16,1536]{2,1,0:T(8,128)S(1)}, f32[4,16,1536]{2,1,0:T(8,128)S(1)}, u32[]{:S(2)}, u32[]{:S(2)}) collective-permute-start(f32[4,16,1536]{2,1,0:T(8,128)S(1)} %get-tuple-element.15), channel_id=1, source_target_pairs={{0,64},{16,24},{8,72},{24,16},{32,96},{48,56},{40,104},{56,48},{64... | collective-permute-start | bytes 1179656 | tf_op jit(solution)/shard_map/ppermute | solution.py:141
  79.4 10.2 %collective-permute-start.3 = (f32[4,16,1536]{2,1,0:T(8,128)S(1)}, f32[4,16,1536]{2,1,0:T(8,128)S(1)}, u32[]{:S(2)}, u32[]{:S(2)}) collective-permute-start(f32[4,16,1536]{2,1,0:T(8,128)S(1)} %get-tuple-element.16), channel_id=1, source_target_pairs={{0,192},{16,56},{8,200},{24,48},{32,224},{48,24},{40,232},{56,16},... | collective-permute-start | bytes 1179656 | tf_op jit(solution)/shard_map/ppermute | solution.py:141
  89.7 5.1 %collective-permute-start.4 = (f32[16,1536]{1,0:T(8,128)S(1)}, f32[16,1536]{1,0:T(8,128)S(1)}, u32[]{:S(2)}, u32[]{:S(2)}) collective-permute-start(f32[16,1536]{1,0:T(8,128)S(1)} %get-tuple-element.17), channel_id=1, source_target_pairs={{0,32},{16,144},{8,40},{24,152},{32,0},{48,176},{40,8},{56,184},{6... | collective-permute-start | bytes 294920 | tf_op jit(solution)/shard_map/ppermute | solution.py:141
  92.4 4.0 %collective-permute-start.5 = (f32[16,1536]{1,0:T(8,128)S(1)}, f32[16,1536]{1,0:T(8,128)S(1)}, u32[]{:S(2)}, u32[]{:S(2)}) collective-permute-start(f32[16,1536]{1,0:T(8,128)S(1)} %get-tuple-element.19), channel_id=1, source_target_pairs={{0,8},{16,80},{8,0},{24,88},{32,40},{48,112},{40,32},{56,120},{64,... | collective-permute-start | bytes 294920 | tf_op jit(solution)/shard_map/ppermute | solution.py:141
  93.1 4.7 %collective-permute-start.6 = (f32[16,1536]{1,0:T(8,128)S(1)}, f32[16,1536]{1,0:T(8,128)S(1)}, u32[]{:S(2)}, u32[]{:S(2)}) collective-permute-start(f32[16,1536]{1,0:T(8,128)S(1)} %get-tuple-element.18), channel_id=1, source_target_pairs={{0,40},{16,208},{8,32},{24,216},{32,8},{48,240},{40,0},{56,248},{6... | collective-permute-start | bytes 294920 | tf_op jit(solution)/shard_map/ppermute | solution.py:141

commit v5 on v4

--- a/solution.py
+++ b/solution.py
@@ -59,39 +59,37 @@
     )(lam)
 
 
-DEPTH = 256
-STEPS = 2304 // DEPTH
+RUNS = [(s, row, min(512, 2304 - row)) for s in range(2) for row in range(0, 2304, 512)]
 
 
 def product_kernel(at_ref, x_ref, w_own_ref, w_oth_ref, *rest):
     outs, (held, acc_ref, sems) = rest[:4], rest[4:]
     copies = []
-    for s, w in enumerate((w_own_ref, w_oth_ref)):
-        for k in range(STEPS):
-            copies.append(pltpu.make_async_copy(w.at[pl.ds(k * DEPTH, DEPTH)], held.at[s, k], sems.at[s, k]))
-            copies[-1].start()
+    for i, (s, row, depth) in enumerate(RUNS):
+        at = pl.ds(row, depth)
+        copies.append(pltpu.make_async_copy((w_own_ref, w_oth_ref)[s].at[at], held.at[s, at], sems.at[i]))
+        copies[-1].start()
     core, y, x_at = at_ref[0], at_ref[1], at_ref[2]
     blocks = [(y ^ (p // 4)) * 4 + ((x_at // 2) ^ (p // 2 % 2)) * 2 + p % 2 for p in range(16)]
     swap = x_at % 2 == 1
 
-    def term(s, k, n):
+    def term(run, n):
+        s, row, depth = run
         x = x_ref.at[core if s == 0 else 1 - core]
-        lhs = jnp.concatenate([x[block, :, k * DEPTH : (k + 1) * DEPTH] for block in blocks], axis=0)
-        return jnp.dot(lhs, held[s, k, :, n : n + 512], preferred_element_type=jnp.float32)
+        lhs = jnp.concatenate([x[block, :, row : row + depth] for block in blocks], axis=0)
+        return jnp.dot(lhs, held[s, row : row + depth, n : n + 512], preferred_element_type=jnp.float32)
 
-    for s in range(2):
-        for k in range(STEPS):
-            copies[s * STEPS + k].wait()
-            if (s, k) == (1, STEPS - 1):
-                break
-            for n in range(0, 1536, 512):
-                if s + k == 0:
-                    acc_ref[:, n : n + 512] = term(s, k, n)
-                else:
-                    acc_ref[:, n : n + 512] += term(s, k, n)
+    for i, run in enumerate(RUNS[:-1]):
+        copies[i].wait()
+        for n in range(0, 1536, 512):
+            if i == 0:
+                acc_ref[:, n : n + 512] = term(run, n)
+            else:
+                acc_ref[:, n : n + 512] += term(run, n)
+    copies[-1].wait()
 
     def total(n):
-        return (0.5 * (acc_ref[:, n : n + 512] + term(1, STEPS - 1, n))).reshape(16, 2, 8, 512)
+        return (0.5 * (acc_ref[:, n : n + 512] + term(RUNS[-1], n))).reshape(16, 2, 8, 512)
 
     for first in range(2):
 
@@ -119,9 +117,9 @@
         out_specs=[pl.BlockSpec(memory_space=pltpu.VMEM)] * 4,
         out_shape=[pltpu.VMEM((4, 16, 1536), jnp.float32)] * 4,
         scratch_shapes=[
-            pltpu.VMEM((2, STEPS, DEPTH, 1536), jnp.bfloat16),
+            pltpu.VMEM((2, 2304, 1536), jnp.bfloat16),
             pltpu.VMEM((256, 1536), jnp.float32),
-            pltpu.SemaphoreType.DMA((2, STEPS)),
+            pltpu.SemaphoreType.DMA((len(RUNS),)),
         ],
         compiler_params=pltpu.CompilerParams(vmem_limit_bytes=20 * MIB),
         cost_estimate=pl.CostEstimate(flops=2 * 256 * 4608 * 1536, bytes_accessed=18 * MIB, transcendentals=0),

time: 114 us -> 114 us (level)
  no operation moved by 1% of the time
where the time goes in v5:
time: 114 us
  waiting for transfers between devices  53.7 us (47%)
  starting transfers between devices  18.1 us (16%)
  blocking collectives  15.3 us (13%)
  local copies, waits for them, and re-layouts  14.3 us (13%)
  Pallas kernels  11.3 us (10%)
    all_to_all x1, waiting for transfers between devices, shards(): received = lax.all_to_all(sent, ('core', 'xl', 'z'), 0, 0)  39.8 us
    all_to_all x1, blocking collectives, shards(): total = lax.all_to_all(total.reshape(16, 2, 768), ('core', 'z'), 0, 0)  15.3 us
    unnamed x2, local copies, waits for them, and re-layouts  14.2 us
    ppermute x6, waiting for transfers between devices, moved(): return lax.ppermute(piece, ('y', 'xh', 'core', 'xl'), pairs(flip, first))  14 us
    all_to_all x1, starting transfers between devices, shards(): received = lax.all_to_all(sent, ('core', 'xl', 'z'), 0, 0)  7.93 us
    ppermute x6, starting transfers between devices, moved(): return lax.ppermute(piece, ('y', 'xh', 'core', 'xl'), pairs(flip, first))  6.82 us
    pallas_call x1, Pallas kernels, product(): pl.pallas_call(product_kernel, in_specs=[pl.BlockSpec(memory_space=pltpu....  6.49 us
    pallas_call x1, Pallas kernels, pack(): pl.pallas_call(pack_kernel, in_specs=[pl.BlockSpec(memory_space=pl.ANY)],...  4.81 us
  transfers between devices with their start and end apart: 8, of which 7 were waited for; matrix products, arithmetic and copies ran while one was open for 13% of the time, Pallas kernels for 0%

profile of v5, /device:TPU:1, one launch (start us, length us, event | category | flops | bytes accessed | tf_op | source)
XLA Modules:
  0.0 113.6 jit_solution(8375080390243531123)
XLA Ops:
  0.0 4.8 %pack.1 = bf16[32,16,2304]{2,1,0:T(8,128)(2,1)} custom-call(bf16[32,48,768]{2,1,0:T(8,128)(2,1)} %lam_ref.1), custom_call_target="tpu_custom_call" | custom-call | flops 603979776 | bytes 4718592 | tf_op jit(solution)/shard_map/pack/pallas_call | solution.py:44
  4.8 3.3 %collective-permute-start = (bf16[48,48,2,768]{3,2,1,0:T(2,128)(2,1)}, bf16[48,48,2,768]{3,2,1,0:T(2,128)(2,1)}, u32[]{:S(2)}, u32[]{:S(2)}) collective-permute-start(bf16[48,48,2,768]{3,2,1,0:T(2,128)(2,1)} %param.3), channel_id=1, source_target_pairs={{0,16},{16,0},{1,17},{17,1},{2,18},{18,2},{3,19},{19,3},{4,20},{20... | collective-permute-start | bytes 21233672 | tf_op jit(solution)/shard_map/ppermute | solution.py:146
  8.1 7.9 %all-to-all-start = ((bf16[32,16,2304]{2,1,0:T(8,128)(2,1)}), bf16[32,16,2304]{2,1,0:T(8,128)(2,1)S(1)}, u32[]{:S(2)}, u32[]{:S(2)}) async-start(bf16[32,16,2304]{2,1,0:T(8,128)(2,1)} %pack.1), calls=%async_computation | async-start | bytes 4718592 | tf_op jit(solution)/shard_map/all_to_all | solution.py:148
  16.1 7.2 %copy.3 = bf16[288,8,2,768]{3,1,2,0:T(8,128)(2,1)} copy(bf16[288,8,2,768]{3,2,1,0:T(2,128)(2,1)} %bitcast.29) | data formatting | bytes 14155776
  23.3 0.1 pad_add_fusion.at_ref
  23.3 0.0 collective-permute-done
  23.4 7.1 %copy.4 = bf16[288,8,2,768]{3,1,2,0:T(8,128)(2,1)} copy(bf16[288,8,2,768]{3,2,1,0:T(2,128)(2,1)} %bitcast.13) | data formatting | bytes 14155776
  30.4 39.8 %all-to-all-done = bf16[32,16,2304]{2,1,0:T(8,128)(2,1)S(1)} async-done(((bf16[32,16,2304]{2,1,0:T(8,128)(2,1)}), bf16[32,16,2304]{2,1,0:T(8,128)(2,1)S(1)}, u32[]{:S(2)}, u32[]{:S(2)}) %all-to-all-start) | async-done | bytes 2359328 | tf_op jit(solution)/shard_map/all_to_all | solution.py:148
  70.2 6.5 %product.1 = (f32[4,16,1536]{2,1,0:T(8,128)S(1)}, f32[4,16,1536]{2,1,0:T(8,128)S(1)}, f32[4,16,1536]{2,1,0:T(8,128)S(1)}, f32[4,16,1536]{2,1,0:T(8,128)S(1)}) custom-call(s32[3]{0:T(128)S(1)} %pad_add_fusion.at_ref, bf16[2,16,16,2304]{3,2,1,0:T(8,128)(2,1)S(1)} %bitcast.26, bf16[2304,1536]{1,0:T(8,128)(2,1)} %bitcast.27, bf16[2304,1536]{1,0:T(8,128)(2,1)} %bitcast.28), custom_call_target="tpu_custom_call" | custom-call | flops 3623878656 | bytes 18874368 | tf_op jit(solution)/shard_map/product/pallas_call | solution.py:109
  76.7 2.5 %collective-permute-start.1 = (f32[4,16,1536]{2,1,0:T(8,128)S(1)}, f32[4,16,1536]{2,1,0:T(8,128)S(1)}, u32[]{:S(2)}, u32[]{:S(2)}) collective-permute-start(f32[4,16,1536]{2,1,0:T(8,128)S(1)} %get-tuple-element.14), channel_id=1, source_target_pairs={{0,128},{16,48},{8,136},{24,56},{32,160},{48,16},{40,168},{56,24},... | collective-permute-start | bytes 1179656 | tf_op jit(solution)/shard_map/ppermute | solution.py:139
  79.2 0.0 collective-permute-start.2
  79.2 0.8 collective-permute-start.3
  80.0 5.2 %collective-permute-done.1 = f32[4,16,1536]{2,1,0:T(8,128)S(1)} collective-permute-done((f32[4,16,1536]{2,1,0:T(8,128)S(1)}, f32[4,16,1536]{2,1,0:T(8,128)S(1)}, u32[]{:S(2)}, u32[]{:S(2)}) %collective-permute-start.1) | collective-permute-done | bytes 393248 | tf_op jit(solution)/shard_map/ppermute | solution.py:139
  85.2 3.0 %collective-permute-done.2 = f32[4,16,1536]{2,1,0:T(8,128)S(1)} collective-permute-done((f32[4,16,1536]{2,1,0:T(8,128)S(1)}, f32[4,16,1536]{2,1,0:T(8,128)S(1)}, u32[]{:S(2)}, u32[]{:S(2)}) %collective-permute-start.2) | collective-permute-done | bytes 393248 | tf_op jit(solution)/shard_map/ppermute | solution.py:139
  88.2 1.2 %collective-permute-done.3 = f32[4,16,1536]{2,1,0:T(8,128)S(1)} collective-permute-done((f32[4,16,1536]{2,1,0:T(8,128)S(1)}, f32[4,16,1536]{2,1,0:T(8,128)S(1)}, u32[]{:S(2)}, u32[]{:S(2)}) %collective-permute-start.3) | collective-permute-done | bytes 393248 | tf_op jit(solution)/shard_map/ppermute | solution.py:139
  89.4 0.1 add_add_fusion
  89.5 2.7 %collective-permute-start.4 = (f32[16,1536]{1,0:T(8,128)S(1)}, f32[16,1536]{1,0:T(8,128)S(1)}, u32[]{:S(2)}, u32[]{:S(2)}) collective-permute-start(f32[16,1536]{1,0:T(8,128)S(1)} %get-tuple-element.17), channel_id=1, source_target_pairs={{0,32},{16,144},{8,40},{24,152},{32,0},{48,176},{40,8},{56,184},{6... | collective-permute-start | bytes 294920 | tf_op jit(solution)/shard_map/ppermute | solution.py:139
  92.2 0.7 collective-permute-start.5
  92.9 0.1 collective-permute-start.6
  93.0 1.6 %collective-permute-done.4 = f32[16,1536]{1,0:T(8,128)S(1)} collective-permute-done((f32[16,1536]{1,0:T(8,128)S(1)}, f32[16,1536]{1,0:T(8,128)S(1)}, u32[]{:S(2)}, u32[]{:S(2)}) %collective-permute-start.4) | collective-permute-done | bytes 98336 | tf_op jit(solution)/shard_map/ppermute | solution.py:139
  94.6 1.7 %collective-permute-done.5 = f32[16,1536]{1,0:T(8,128)S(1)} collective-permute-done((f32[16,1536]{1,0:T(8,128)S(1)}, f32[16,1536]{1,0:T(8,128)S(1)}, u32[]{:S(2)}, u32[]{:S(2)}) %collective-permute-start.5) | collective-permute-done | bytes 98336 | tf_op jit(solution)/shard_map/ppermute | solution.py:139
  96.2 1.3 %collective-permute-done.6 = f32[16,1536]{1,0:T(8,128)S(1)} collective-permute-done((f32[16,1536]{1,0:T(8,128)S(1)}, f32[16,1536]{1,0:T(8,128)S(1)}, u32[]{:S(2)}, u32[]{:S(2)}) %collective-permute-start.6) | collective-permute-done | bytes 98336 | tf_op jit(solution)/shard_map/ppermute | solution.py:139
  97.6 0.1 reshape.18
  97.7 15.3 %all_to_all.10 = f32[16,2,768]{2,1,0:T(2,128)S(1)} all-to-all(f32[16,2,768]{2,1,0:T(2,128)S(1)} %reshape.18), channel_id=1, replica_groups=mesh['y'=4,'xh'=2,'core'=2,'xl'=2,'z'=8] {'core','z'}, dimensions={0} | all-to-all | bytes 196608 | tf_op jit(solution)/shard_map/all_to_all | solution.py:157
  113.0 0.6 bitcast_reduce_fusion
  (2 shorter events, 0.1 us)
Async XLA Ops:
  4.8 18.5 %collective-permute-start = (bf16[48,48,2,768]{3,2,1,0:T(2,128)(2,1)}, bf16[48,48,2,768]{3,2,1,0:T(2,128)(2,1)}, u32[]{:S(2)}, u32[]{:S(2)}) collective-permute-start(bf16[48,48,2,768]{3,2,1,0:T(2,128)(2,1)} %param.3), channel_id=1, source_target_pairs={{0,16},{16,0},{1,17},{17,1},{2,18},{18,2},{3,19},{19,3},{4,20},{20... | collective-permute-start | bytes 21233672 | tf_op jit(solution)/shard_map/ppermute | solution.py:146
  8.1 62.0 %all-to-all-start = ((bf16[32,16,2304]{2,1,0:T(8,128)(2,1)}), bf16[32,16,2304]{2,1,0:T(8,128)(2,1)S(1)}, u32[]{:S(2)}, u32[]{:S(2)}) async-start(bf16[32,16,2304]{2,1,0:T(8,128)(2,1)} %pack.1), calls=%async_computation | async-start | bytes 4718592 | tf_op jit(solution)/shard_map/all_to_all | solution.py:148
  76.7 8.6 %collective-permute-start.1 = (f32[4,16,1536]{2,1,0:T(8,128)S(1)}, f32[4,16,1536]{2,1,0:T(8,128)S(1)}, u32[]{:S(2)}, u32[]{:S(2)}) collective-permute-start(f32[4,16,1536]{2,1,0:T(8,128)S(1)} %get-tuple-element.14), channel_id=1, source_target_pairs={{0,128},{16,48},{8,136},{24,56},{32,160},{48,16},{40,168},{56,24},... | collective-permute-start | bytes 1179656 | tf_op jit(solution)/shard_map/ppermute | solution.py:139
  79.2 9.0 %collective-permute-start.2 = (f32[4,16,1536]{2,1,0:T(8,128)S(1)}, f32[4,16,1536]{2,1,0:T(8,128)S(1)}, u32[]{:S(2)}, u32[]{:S(2)}) collective-permute-start(f32[4,16,1536]{2,1,0:T(8,128)S(1)} %get-tuple-element.15), channel_id=1, source_target_pairs={{0,64},{16,24},{8,72},{24,16},{32,96},{48,56},{40,104},{56,48},{64... | collective-permute-start | bytes 1179656 | tf_op jit(solution)/shard_map/ppermute | solution.py:139
  79.2 10.2 %collective-permute-start.3 = (f32[4,16,1536]{2,1,0:T(8,128)S(1)}, f32[4,16,1536]{2,1,0:T(8,128)S(1)}, u32[]{:S(2)}, u32[]{:S(2)}) collective-permute-start(f32[4,16,1536]{2,1,0:T(8,128)S(1)} %get-tuple-element.16), channel_id=1, source_target_pairs={{0,192},{16,56},{8,200},{24,48},{32,224},{48,24},{40,232},{56,16},... | collective-permute-start | bytes 1179656 | tf_op jit(solution)/shard_map/ppermute | solution.py:139
  89.5 5.1 %collective-permute-start.4 = (f32[16,1536]{1,0:T(8,128)S(1)}, f32[16,1536]{1,0:T(8,128)S(1)}, u32[]{:S(2)}, u32[]{:S(2)}) collective-permute-start(f32[16,1536]{1,0:T(8,128)S(1)} %get-tuple-element.17), channel_id=1, source_target_pairs={{0,32},{16,144},{8,40},{24,152},{32,0},{48,176},{40,8},{56,184},{6... | collective-permute-start | bytes 294920 | tf_op jit(solution)/shard_map/ppermute | solution.py:139
  92.2 4.0 %collective-permute-start.5 = (f32[16,1536]{1,0:T(8,128)S(1)}, f32[16,1536]{1,0:T(8,128)S(1)}, u32[]{:S(2)}, u32[]{:S(2)}) collective-permute-start(f32[16,1536]{1,0:T(8,128)S(1)} %get-tuple-element.19), channel_id=1, source_target_pairs={{0,8},{16,80},{8,0},{24,88},{32,40},{48,112},{40,32},{56,120},{64,... | collective-permute-start | bytes 294920 | tf_op jit(solution)/shard_map/ppermute | solution.py:139
  92.9 4.7 %collective-permute-start.6 = (f32[16,1536]{1,0:T(8,128)S(1)}, f32[16,1536]{1,0:T(8,128)S(1)}, u32[]{:S(2)}, u32[]{:S(2)}) collective-permute-start(f32[16,1536]{1,0:T(8,128)S(1)} %get-tuple-element.18), channel_id=1, source_target_pairs={{0,40},{16,208},{8,32},{24,216},{32,8},{48,240},{40,0},{56,248},{6... | collective-permute-start | bytes 294920 | tf_op jit(solution)/shard_map/ppermute | solution.py:139
